TPU v7x, 256 devices: a whole 4x4x8 slice. The times are simulated.
256 devices in a mesh: row: 2 (over core), col: 8 (over z), depth: 16 (over y, x).
Axes of the slice: x: 4, y: 4, z: 8, core: 2. Of those that a mesh axis runs over, the one named last changes fastest.
Arguments:
- tokens: bfloat16 [2560, 4096], P(('depth', 'col'), 'row'), may hold values from -6 to 6
- gate_weight: bfloat16 [4096, 14336], P('row', 'col'), may hold values from -0.09375 to 0.09375
- up_weight: bfloat16 [4096, 14336], P('row', 'col'), may hold values from -0.09375 to 0.09375
- down_weight: bfloat16 [14336, 4096], P('col', 'row'), may hold values from -0.046875 to 0.046875
- cotangent: bfloat16 [2560, 4096], P(('depth', 'col'), 'row'), may hold values from -6 to 6
Outputs:
- layer_out: bfloat16 [2560, 4096], P(('depth', 'col'), 'row')
- input_grad: bfloat16 [2560, 4096], P(('depth', 'col'), 'row')
- gate_grad_w: bfloat16 [4096, 14336], P(('row', 'depth'), 'col')
- up_grad_w: bfloat16 [4096, 14336], P(('row', 'depth'), 'col')
- down_grad_w: bfloat16 [14336, 4096], P('col', ('row', 'depth'))
All inputs are finite; a program needn't handle non-finite values.
Results may differ from a plain program's by a relative error of at most 0.0049.
Values may be sent and summed in bfloat16 or wider, within the bound.
No kernel may reach another device: no remote copies, remote signals or barrier semaphores. Data moves between devices by JAX's collectives and lax.ppermute only.
A program may use at most 192 MiB of HBM per device.

v0:
```python
import functools

import jax
import jax.numpy as jnp
from jax import lax
from jax.experimental import pallas as pl
from jax.experimental.pallas import tpu as pltpu
from jax.sharding import PartitionSpec as P

BF = jnp.bfloat16
F32 = jnp.float32
COLS, SIDE, LANES = 8, 4, 128
ALONG_X = [[SIDE * y + x for x in range(SIDE)] for y in range(SIDE)]
ALONG_Y = [[SIDE * y + x for y in range(SIDE)] for x in range(SIDE)]
MIB = 1 << 20
CHUNK = 512


def dot(left, right, dims):
    return lax.dot_general(left, right, (dims, ((), ())), preferred_element_type=F32)


def to_z(value, step):
    return lax.ppermute(value, "col", [(k, (k + step) % COLS) for k in range(COLS)])


def to_x(value, step):
    pairs = [(k, k // SIDE * SIDE + (k + step) % SIDE) for k in range(SIDE * SIDE)]
    return lax.ppermute(value, "depth", pairs)


def to_y(value, step):
    side = SIDE * SIDE
    return lax.ppermute(value, "depth", [(k, (k + SIDE * step) % side) for k in range(side)])


def to_core(value):
    return lax.ppermute(value, "row", [(0, 1), (1, 0)])


def swap(value, groups):
    return lax.all_to_all(
        value, "depth", split_axis=0, concat_axis=0, axis_index_groups=groups, tiled=True
    )


def shape(*dims, dtype=BF):
    return jax.ShapeDtypeStruct(dims, dtype)


def hbm(*values):
    return [pltpu.with_memory_space_constraint(value, pltpu.HBM) for value in values]


def cost(flops, moved):
    return pl.CostEstimate(flops=flops, bytes_accessed=moved, transcendentals=0)


def call(kernel, outs, *args, limit=16, scratch=()):
    return pl.pallas_call(
        kernel,
        out_shape=outs,
        scratch_shapes=list(scratch),
        compiler_params=pltpu.CompilerParams(vmem_limit_bytes=limit * MIB),
    )(*args)


def assemble(blocks, feat, upst, send_a, send_b, feat32, upst32):
    rows = blocks[0].shape[0] // 2
    width = feat.shape[1]
    for k in range(COLS):
        if k < COLS // 2:
            block = blocks[k][...].astype(F32)
        elif k == COLS // 2:
            block = jnp.concatenate([blocks[k][...], blocks[k + 1][...]], axis=1).astype(F32)
        else:
            block = blocks[k + 1][...].astype(F32)
        feat32[pl.ds(rows * k, rows), :] = block[:rows]
        upst32[pl.ds(rows * k, rows), :] = block[rows:]
    feat[...] = feat32[...].astype(BF)
    upst[...] = upst32[...].astype(BF)
    quarter = width // SIDE
    for i in range(SIDE):
        send_b[i] = feat[:, quarter * i : quarter * (i + 1)]
        for j in range(SIDE):
            column = LANES * (SIDE * j + i)
            send_a[i, :, LANES * j : LANES * (j + 1)] = feat[:, column : column + LANES]
            send_a[i, :, quarter + LANES * j : quarter + LANES * (j + 1)] = upst[
                :, column : column + LANES
            ]


def gather_col(value):
    half = value.shape[1] // 2
    before, after = to_z(value, 1), to_z(value, -1)
    before2, after2 = to_z(value, 2), to_z(value, -2)
    before3, after3 = to_z(before2, 1), to_z(after2, -1)
    far = (to_z(before2[:, :half], 2), to_z(after2[:, half:], -2))
    return [value, after, after2, after3, *far, before3, before2, before]


def started(moves, sems):
    copies = [pltpu.make_async_copy(*move, sems.at[k]) for k, move in enumerate(moves)]
    for copy in copies:
        copy.start()
    return copies


def weight_copies(which, weights, targets, sems):
    model, half = targets[0].shape
    own = pl.ds(pl.multiple_of(which[0] * half, LANES), half)

    def pair(k):
        at = pl.ds(pl.multiple_of(CHUNK * k, CHUNK), CHUNK)
        return [
            pltpu.make_async_copy(weights[j].at[at, own], targets[j].at[at], sems.at[2 * k + j])
            for j in range(2)
        ]

    last = pltpu.make_async_copy(weights[2].at[own], targets[2], sems.at[2 * model // CHUNK])
    for k in range(model // CHUNK):
        for copy in pair(k):
            copy.start()
    last.start()
    return pair, last


def products(copies, feat, upst, weights, out):
    model, half = weights[0].shape
    pair, last = copies
    out[:, : 2 * half] = jnp.zeros((out.shape[0], 2 * half), F32)

    def step(k, carry):
        at = pl.ds(pl.multiple_of(CHUNK * k, CHUNK), CHUNK)
        for j, copy in enumerate(pair(k)):
            copy.wait()
            place = slice(half * j, half * (j + 1))
            out[:, place] += dot(feat[:, at], weights[j][at, :], ((1,), (0,)))
        return carry

    lax.fori_loop(0, model // CHUNK, step, 0)
    last.wait()
    out[:, 2 * half :] = dot(upst[...], weights[2][...], ((1,), (1,)))


def first_kernel(which, *refs):
    blocks, weights, outs = refs[: COLS + 1], refs[COLS + 1 : COLS + 4], refs[COLS + 4 : COLS + 9]
    out, *assembled = outs
    *targets, feat32, upst32, sems = refs[COLS + 9 :]
    copies = weight_copies(which, weights, targets, sems)
    assemble(blocks, *assembled, feat32, upst32)
    products(copies, *assembled[:2], targets, out)


def second_kernel(which, feat, upst, gate, up, down, out, *scratch):
    targets, sems = scratch[:3], scratch[3]
    copies = weight_copies(which, (gate, up, down), targets, sems)
    products(copies, feat, upst, targets, out)


def in_hbm(kernel, outs, which, vmem, operands, scratch, copies, work, limit):
    return pl.pallas_call(
        kernel,
        in_specs=[pl.BlockSpec(memory_space=pltpu.SMEM)]
        + [pl.BlockSpec(memory_space=pltpu.VMEM)] * len(vmem)
        + [pl.BlockSpec(memory_space=pl.ANY)] * len(operands),
        out_specs=jax.tree.map(
            lambda out: (
                pl.BlockSpec(memory_space=pltpu.VMEM)
                if isinstance(out, jax.ShapeDtypeStruct)
                else pl.BlockSpec()
            ),
            outs,
        ),
        out_shape=outs,
        scratch_shapes=[pltpu.VMEM(*s) for s in scratch] + [pltpu.SemaphoreType.DMA((copies,))],
        cost_estimate=cost(*work),
        compiler_params=pltpu.CompilerParams(vmem_limit_bytes=limit * MIB),
    )(which, *vmem, *hbm(*operands))


def project(which, arrays, weights, rows=None):
    model, units = weights[0].shape
    half = units // 2
    group = COLS * rows if rows else arrays[0].shape[0]
    outs = [shape(group, 3 * half, dtype=F32)]
    scratch = [((model, half), BF)] * 2 + [((half, model), BF)]
    if rows:
        width = SIDE * LANES
        outs += [shape(group, model)] * 2
        outs += [pltpu.HBM((SIDE, group, n), BF) for n in (2 * width, width)]
        scratch += [((group, model), F32)] * 2
    return in_hbm(
        first_kernel if rows else second_kernel,
        outs,
        jnp.reshape(which, (1,)),
        arrays,
        weights,
        scratch,
        2 * model // CHUNK + 1,
        (0, 0),
        28,
    )


def swiglu_kernel(own, theirs, route_a, route_b, grads):
    half = own.shape[1] // 3
    cut = route_a.shape[1] - half
    parts = [slice(half * k, half * (k + 1)) for k in range(3)]
    gate_pre = own[:, parts[0]] + theirs[:, parts[0]]
    up_pre = own[:, parts[1]] + theirs[:, parts[1]]
    hidden_grad = own[:, parts[2]] + theirs[:, parts[2]]
    logistic = jax.nn.sigmoid(gate_pre)
    hidden = (gate_pre * logistic * up_pre).astype(BF)
    gate_grad = hidden_grad * up_pre * logistic * (1.0 + gate_pre * (1.0 - logistic))
    gate_grad = gate_grad.astype(BF)
    up_grad = (hidden_grad * gate_pre * logistic).astype(BF)
    route_a[:, :half] = hidden
    route_a[:, half:] = gate_grad[:, :cut]
    route_b[:, : half - cut] = gate_grad[:, cut:]
    route_b[:, half - cut :] = up_grad
    for part, value in zip(parts, (gate_grad, up_grad, hidden)):
        grads[:, part] = value


def whole_moves(place, half, own, theirs, parts, targets):
    moves = []
    for part, target in zip(parts, targets):
        for source, which in ((own, place[0]), (theirs, 1 - place[0])):
            at = pl.ds(pl.multiple_of(which * half, LANES), half)
            moves.append((source.at[:, pl.ds(half * part, half)], target.at[:, at]))
    return moves


def store_blocks(place, out, total, base):
    rows, width = out.shape[1], total.shape[1]
    for k in range(COLS):
        at = lax.rem(place[1] + k, COLS)
        out[at, :, base : base + width] = total[pl.ds(rows * k, rows), :].astype(BF)


def forward_kernel(place, theirs, own, down, out, hidden, down_v, total, sems):
    units = down.shape[0]
    size = CHUNK // 2
    moves = whole_moves(place, units // 2, own, theirs, (2,), (hidden,))
    copies = started(moves, sems)

    def part(k):
        at = pl.ds(pl.multiple_of(size * k, size), size)
        return pltpu.make_async_copy(down.at[at], down_v.at[at], sems.at[2 + k])

    for k in range(units // size):
        part(k).start()
    total[...] = jnp.zeros(total.shape, F32)
    for copy in copies:
        copy.wait()

    def step(k, carry):
        part(k).wait()
        at = pl.ds(pl.multiple_of(size * k, size), size)
        total[...] += dot(hidden[:, at], down_v[at, :], ((1,), (0,)))
        return carry

    lax.fori_loop(0, units // size, step, 0)
    store_blocks(place, out, total, 0)


def backward_kernel(
    place, first, theirs, own, gate, up, out, gate_g, up_g, gate_v, up_v, total, sems
):
    model, units = gate.shape
    moves = whole_moves(place, units // 2, own, theirs, (0, 1), (gate_g, up_g))
    moves.append((first, out.at[:, :, pl.ds(0, model)]))
    copies = started(moves, sems)

    def pair(k):
        at = pl.ds(pl.multiple_of(CHUNK * k, CHUNK), CHUNK)
        return [
            pltpu.make_async_copy(source.at[at], target.at[at], sems.at[5 + 2 * k + j])
            for j, (source, target) in enumerate(((gate, gate_v), (up, up_v)))
        ]

    for k in range(model // CHUNK):
        for copy in pair(k):
            copy.start()
    for copy in copies:
        copy.wait()

    def step(k, carry):
        for copy in pair(k):
            copy.wait()
        at = pl.ds(pl.multiple_of(CHUNK * k, CHUNK), CHUNK)
        product = dot(gate_g[...], gate_v[at, :], ((1,), (1,)))
        total[:, at] = product + dot(up_g[...], up_v[at, :], ((1,), (1,)))
        return carry

    lax.fori_loop(0, model // CHUNK, step, 0)
    store_blocks(place, out, total, model)


def forward(place, grads, down_weight, rows):
    units, model = down_weight.shape
    group = COLS * rows
    return in_hbm(
        forward_kernel,
        shape(COLS, rows, model),
        place,
        grads[1:],
        (grads[0], down_weight),
        [((group, units), BF), ((units, model), BF), ((group, model), F32)],
        2 + 2 * units // CHUNK,
        (2 * group * model * units, 2 * model * units),
        16,
    )


def backward(place, grads, gate_weight, up_weight, first, rows):
    model, units = gate_weight.shape
    group = COLS * rows
    return in_hbm(
        backward_kernel,
        shape(COLS, rows, 2 * model),
        place,
        (first, grads[1]),
        (grads[0], gate_weight, up_weight),
        [((group, units), BF)] * 2 + [((model, units), BF)] * 2 + [((group, model), F32)],
        5 + 2 * model // CHUNK,
        (4 * group * model * units, 4 * model * units),
        28,
    )


def weight_kernel(cut, place, *refs):
    pieces = (*refs[1:4], refs[0])
    own, before, after, far_a, far_b, piece, columns, sems = refs[6:]
    group, wide = pieces[0].shape
    width = SIDE * LANES
    around = (0, SIDE - 1, 1, 2)
    moves = [(pieces[s], piece.at[pl.ds(group * s, group)]) for s in range(SIDE)]
    moves += [(refs[4 + t], columns.at[t]) for t in range(2)]
    sources = [lax.rem(place[0] + offset, SIDE) for offset in around]
    for copy in started(moves, sems):
        copy.wait()
    for ref, offset in ((far_a, 2), (after, 1), (before, SIDE - 1), (own, 0)):
        start = LANES * lax.rem(place[1] + offset, SIDE)
        for first, last, base in ((0, cut, width), (cut, wide, 0)):
            if first == last:
                continue
            at = pl.ds(pl.multiple_of(base + start, LANES), LANES)
            left = jnp.concatenate(
                [
                    jnp.concatenate([columns[t, source, :, at] for t in range(2)], axis=1)
                    for source in sources
                ],
                axis=0,
            )
            value = dot(left, piece[:, first:last], ((0,), (0,)))
            if ref is far_a:
                far_a[:, first:last] = value[:LANES].astype(BF)
                far_b[:, first:last] = value[LANES:].astype(BF)
            else:
                ref[:, first:last] = value.astype(ref.dtype)


def weight_partials(cut, place, pieces, columns):
    group, wide = pieces[0].shape
    tokens, width = SIDE * group, columns[0].shape[2]
    return in_hbm(
        functools.partial(weight_kernel, cut),
        [shape(2 * LANES, wide, dtype=F32)]
        + [shape(2 * LANES, wide)] * 2
        + [shape(LANES, wide)] * 2,
        place,
        pieces[3:],
        (*pieces[:3], *columns),
        [((tokens, wide), BF), ((2, *columns[0].shape), BF)],
        SIDE + 2,
        (16 * tokens * LANES * wide, 2 * tokens * (wide + 2 * width)),
        20,
    )


def pass_on_kernel(before, after, from_before, from_after, send_before, send_after):
    first, second = pl.ds(0, LANES), pl.ds(LANES, LANES)
    total = after[first, :].astype(F32) + from_before[...].astype(F32)
    send_after[first, :] = total.astype(BF)
    send_after[second, :] = after[second, :]
    send_before[first, :] = before[first, :]
    total = before[second, :].astype(F32) + from_after[...].astype(F32)
    send_before[second, :] = total.astype(BF)


def sum_kernel(own, from_before, from_after, mine, theirs):
    total = own[...] + from_before[...].astype(F32) + from_after[...].astype(F32)
    mine[...] = total[:LANES].astype(BF)
    theirs[...] = total[LANES:].astype(BF)


def scatter(cut, place, pieces, columns, send):
    wide = pieces[0].shape[1]
    own, before, after, far_a, far_b = weight_partials(cut, place, pieces, columns)
    from_before, from_after = send(far_a, 1), send(far_b, -1)
    pair = [shape(2 * LANES, wide)] * 2
    send_before, send_after = call(pass_on_kernel, pair, before, after, from_before, from_after)
    return own, send(send_after, 1), send(send_before, -1)


def finish_kernel(which, mine_a, other_a, mine_b, other_b, gate, up, down):
    half = gate.shape[1] // 2
    cut = mine_a.shape[1] - half
    rest = half - cut

    def place(a, b, base):
        gate[:, base : base + cut] = a[:, half:]
        gate[:, base + cut : base + half] = b[:, :rest]
        up[:, base : base + half] = b[:, rest:]
        down[base : base + half, :] = a[:, :half].T

    @pl.when(which[0] == 0)
    def _():
        place(mine_a, mine_b, 0)
        place(other_a, other_b, half)

    @pl.when(which[0] != 0)
    def _():
        place(other_a, other_b, 0)
        place(mine_a, mine_b, half)


def total_kernel(moved, out, grad):
    model = out.shape[1]
    total = moved[0].astype(F32)
    for k in range(1, COLS):
        total = total + moved[k].astype(F32)
    out[...] = total[:, :model].astype(BF)
    grad[...] = total[:, model:].astype(BF)


def call_at(kernel, outs, which, *args):
    return pl.pallas_call(
        kernel,
        in_specs=[pl.BlockSpec(memory_space=pltpu.SMEM)]
        + [pl.BlockSpec(memory_space=pltpu.VMEM)] * len(args),
        out_shape=outs,
        compiler_params=pltpu.CompilerParams(vmem_limit_bytes=16 * MIB),
    )(which, *args)


def gather(value, send):
    before, after = send(value, 1), send(value, -1)
    return [value, before, after, send(before, 1)]


def body(tokens, gate_weight, up_weight, down_weight, cotangent):
    row, col, depth = (lax.axis_index(name) for name in ("row", "col", "depth"))
    at_x, at_y = depth % SIDE, depth // SIDE
    rows, model = tokens.shape
    group = rows * COLS
    half = gate_weight.shape[1] // 2
    cut = (half // LANES // 2 + 1) * LANES

    blocks = gather_col(jnp.concatenate([tokens, cotangent], axis=0))
    weights = (gate_weight, up_weight, down_weight)
    sent, features, upstream, send_a, send_b = project(1 - row, blocks, weights, rows)
    (kept,) = project(row, (features, upstream), weights)
    route_a, route_b, grads = call(
        swiglu_kernel,
        [pltpu.HBM((group, n), BF) for n in (half + cut, 2 * half - cut, 3 * half)],
        kept,
        *hbm(to_core(sent)),
    )
    columns_a = swap(send_a, ALONG_X)

    grads = (grads, to_core(grads))
    before_a, after_a = to_x(route_a, 1), to_x(route_a, -1)
    before_b, after_b = to_y(route_b, 1), to_y(route_b, -1)
    place = jnp.stack([row, col])
    first = forward(place, grads, down_weight, rows)
    columns_a, send_b, first = lax.optimization_barrier((columns_a, send_b, first))
    columns_b = swap(send_b, ALONG_Y)
    columns_a = (columns_a, to_core(columns_a))
    columns_b = (columns_b, to_core(columns_b))

    before_a, after_b, first = lax.optimization_barrier((before_a, after_b, first))
    grads, _ = lax.optimization_barrier((grads, (before_a, before_b, after_a, after_b)))
    part = backward(place, grads, gate_weight, up_weight, first, rows)
    wide_a = [route_a, before_a, after_a, to_x(before_a, 1)]
    wide_b = [route_b, before_b, after_b, to_y(after_b, -1)]
    wide_a[1], wide_b[1], part = lax.optimization_barrier((wide_a[1], wide_b[1], part))
    part, _ = lax.optimization_barrier((part, (wide_a[3], wide_b[3])))
    moved = lax.all_to_all(part, "col", split_axis=0, concat_axis=0, tiled=True)
    layer_out, input_grad = call(total_kernel, [shape(rows, model)] * 2, moved)

    moved_a = scatter(half, jnp.stack([at_x, at_y]), wide_a, columns_a, to_y)
    moved_b = scatter(0, jnp.stack([at_y, at_x]), wide_b, columns_b, to_x)
    pair = [shape(LANES, moved_a[0].shape[1])] * 2
    moved_a, layer_out = lax.optimization_barrier((moved_a, layer_out))
    mine_a, other_a = call(sum_kernel, pair, *moved_a)
    pair = [shape(LANES, moved_b[0].shape[1])] * 2
    mine_b, other_b = call(sum_kernel, pair, *moved_b)
    weight_grads = call_at(
        finish_kernel,
        [shape(LANES, 2 * half)] * 2 + [shape(2 * half, LANES)],
        jnp.reshape(row, (1,)),
        mine_a,
        to_core(other_a),
        mine_b,
        to_core(other_b),
    )
    return (layer_out, input_grad, *weight_grads)


def solution(mesh):
    in_specs = (
        P(("depth", "col"), "row"),
        P("row", "col"),
        P("row", "col"),
        P("col", "row"),
        P(("depth", "col"), "row"),
    )
    out_specs = (
        P(("depth", "col"), "row"),
        P(("depth", "col"), "row"),
        P(("row", "depth"), "col"),
        P(("row", "depth"), "col"),
        P("col", ("row", "depth")),
    )
    return jax.shard_map(body, mesh=mesh, in_specs=in_specs, out_specs=out_specs, check_vma=False)
```

profile of v0, /device:TPU:1, one launch (start us, length us, event | category | flops | bytes accessed | tf_op | source)
XLA Modules:
  0.0 137.2 jit_solution(11658024146882708190)
XLA Ops:
  0.6 1.0 pad_maximum_fusion.refs_0_
  1.6 3.9 %collective-permute-start.3 = (bf16[40,2048]{1,0:T(8,128)(2,1)S(1)}, bf16[40,2048]{1,0:T(8,128)(2,1)S(1)}, u32[]{:S(2)}, u32[]{:S(2)}) collective-permute-start(bf16[40,2048]{1,0:T(8,128)(2,1)S(1)} %pad_maximum_fusion.refs_0_), channel_id=1, source_target_pairs={{0,32},{16,48},{32,64},{48,80},{64,96},{80,112},{96,0},{112,16},{1... | collective-permute-start | bytes 491528 | tf_op jit(solution)/shard_map/ppermute | solution.py:24
  5.5 3.1 %collective-permute-start.1 = (bf16[40,2048]{1,0:T(8,128)(2,1)S(1)}, bf16[40,2048]{1,0:T(8,128)(2,1)S(1)}, u32[]{:S(2)}, u32[]{:S(2)}) collective-permute-start(bf16[40,2048]{1,0:T(8,128)(2,1)S(1)} %pad_maximum_fusion.refs_0_), channel_id=1, source_target_pairs={{0,96},{16,112},{32,0},{48,16},{64,32},{80,48},{96,64},{112,80},{1... | collective-permute-start | bytes 491528 | tf_op jit(solution)/shard_map/ppermute | solution.py:24
  8.6 0.7 collective-permute-start.7
  9.4 1.9 %collective-permute-start = (bf16[40,2048]{1,0:T(8,128)(2,1)S(1)}, bf16[40,2048]{1,0:T(8,128)(2,1)S(1)}, u32[]{:S(2)}, u32[]{:S(2)}) collective-permute-start(bf16[40,2048]{1,0:T(8,128)(2,1)S(1)} %pad_maximum_fusion.refs_0_), channel_id=1, source_target_pairs={{0,112},{16,0},{32,16},{48,32},{64,48},{80,64},{96,80},{112,96},{1... | collective-permute-start | bytes 491528 | tf_op jit(solution)/shard_map/ppermute | solution.py:24
  11.3 1.7 %collective-permute-done.3.refs_7_ = bf16[40,2048]{1,0:T(8,128)(2,1)S(1)} collective-permute-done((bf16[40,2048]{1,0:T(8,128)(2,1)S(1)}, bf16[40,2048]{1,0:T(8,128)(2,1)S(1)}, u32[]{:S(2)}, u32[]{:S(2)}) %collective-permute-start.3) | collective-permute-done | bytes 163872 | tf_op jit(solution)/shard_map/ppermute | solution.py:24
  13.0 3.9 %collective-permute-start.6 = (bf16[40,2048]{1,0:T(8,128)(2,1)S(1)}, bf16[40,2048]{1,0:T(8,128)(2,1)S(1)}, u32[]{:S(2)}, u32[]{:S(2)}) collective-permute-start(bf16[40,2048]{1,0:T(8,128)(2,1)S(1)} %collective-permute-done.3.refs_7_), channel_id=1, source_target_pairs={{0,16},{16,32},{32,48},{48,64},{64,80},{80,96},{96,112},{112,0},{1... | collective-permute-start | bytes 491528 | tf_op jit(solution)/shard_map/ppermute | solution.py:24
  17.5 2.6 %collective-permute-start.4 = (bf16[40,1024]{1,0:T(8,128)(2,1)S(1)}, bf16[40,1024]{1,0:T(8,128)(2,1)S(1)}, u32[]{:S(2)}, u32[]{:S(2)}) collective-permute-start(bf16[40,1024]{1,0:T(8,128)(2,1)S(1)} %slice.8), channel_id=1, source_target_pairs={{0,32},{16,48},{32,64},{48,80},{64,96},{80,112},{96,0},{112,16},{1... | collective-permute-start | bytes 245768 | tf_op jit(solution)/shard_map/ppermute | solution.py:24
  20.0 1.6 %collective-permute-start.5 = (bf16[40,1024]{1,0:T(8,128)(2,1)S(1)}, bf16[40,1024]{1,0:T(8,128)(2,1)S(1)}, u32[]{:S(2)}, u32[]{:S(2)}) collective-permute-start(bf16[40,1024]{1,0:T(8,128)(2,1)S(1)} %slice.9), channel_id=1, source_target_pairs={{0,96},{16,112},{32,0},{48,16},{64,32},{80,48},{96,64},{112,80},{1... | collective-permute-start | bytes 245768 | tf_op jit(solution)/shard_map/ppermute | solution.py:24
  21.7 2.3 %collective-permute-done.4.refs_4_ = bf16[40,1024]{1,0:T(8,128)(2,1)S(1)} collective-permute-done((bf16[40,1024]{1,0:T(8,128)(2,1)S(1)}, bf16[40,1024]{1,0:T(8,128)(2,1)S(1)}, u32[]{:S(2)}, u32[]{:S(2)}) %collective-permute-start.4) | collective-permute-done | bytes 81952 | tf_op jit(solution)/shard_map/ppermute | solution.py:24
  24.0 3.2 %collective-permute-done.5.refs_5_ = bf16[40,1024]{1,0:T(8,128)(2,1)S(1)} collective-permute-done((bf16[40,1024]{1,0:T(8,128)(2,1)S(1)}, bf16[40,1024]{1,0:T(8,128)(2,1)S(1)}, u32[]{:S(2)}, u32[]{:S(2)}) %collective-permute-start.5) | collective-permute-done | bytes 81952 | tf_op jit(solution)/shard_map/ppermute | solution.py:24
  27.2 6.9 %shard_map.92 = (f32[160,2688]{1,0:T(8,128)}, bf16[160,2048]{1,0:T(8,128)(2,1)S(1)}, bf16[160,2048]{1,0:T(8,128)(2,1)S(1)}, bf16[4,160,1024]{2,1,0:T(8,128)(2,1)}, bf16[4,160,512]{2,1,0:T(8,128)(2,1)}) custom-call(s32[1]{0:T(128)} %bitcast.3.which, bf16[40,2048]{1,0:T(8,128)(2,1)S(1)} %pad_maximum_fusion.refs_0_, ...), custom_call_target="tpu_custom_call" | custom-call | tf_op jit(solution)/shard_map/pallas_call | solution.py:162
  34.1 2.0 %collective-permute-start.8 = (f32[160,2688]{1,0:T(8,128)}, f32[160,2688]{1,0:T(8,128)S(1)}, u32[]{:S(2)}, u32[]{:S(2)}) collective-permute-start(f32[160,2688]{1,0:T(8,128)} %get-tuple-element.54), channel_id=1, source_target_pairs={{0,128},{128,0},{1,129},{129,1},{2,130},{130,2},{3,131},{131,3},{4... | collective-permute-start | bytes 5160968 | tf_op jit(solution)/shard_map/ppermute | solution.py:38
  36.1 4.3 %all-to-all-start = ((bf16[4,160,1024]{2,1,0:T(8,128)(2,1)}), bf16[4,160,1024]{2,1,0:T(8,128)(2,1)}, u32[]{:S(2)}, u32[]{:S(2)}) async-start(bf16[4,160,1024]{2,1,0:T(8,128)(2,1)} %get-tuple-element.57), calls=%async_computation | async-start | bytes 2621440 | tf_op jit(solution)/shard_map/all_to_all | solution.py:42
  40.4 5.7 %shard_map.93.own = f32[160,2688]{1,0:T(8,128)S(1)} custom-call(s32[1]{0:T(128)} %bitcast.2.which, bf16[160,2048]{1,0:T(8,128)(2,1)S(1)} %get-tuple-element.52.feat, bf16[160,2048]{1,0:T(8,128)(2,1)S(1)} %get-tuple-element.53.upst, bf16[2048,1792]{1,0:T(8,128)(2,1)} %gate.3, bf16[2048,1792]{1,0:T(8,128)(2,1)} %up.3, bf16[1792,2048]{1,0:T(8,128)(2,1)} %down.3), custom_call_target="tpu_custom_call" | custom-call | tf_op jit(solution)/shard_map/pallas_call | solution.py:162
  46.2 1.2 copy-done.4
  47.4 3.0 %shard_map.94 = (bf16[160,1408]{1,0:T(8,128)(2,1)}, bf16[160,1280]{1,0:T(8,128)(2,1)}, bf16[160,2688]{1,0:T(8,128)(2,1)}) custom-call(f32[160,2688]{1,0:T(8,128)S(1)} %shard_map.93.own, f32[160,2688]{1,0:T(8,128)} %copy-done.4), custom_call_target="tpu_custom_call" | custom-call | tf_op jit(solution)/shard_map/pallas_call | solution.py:60
  50.4 1.7 %collective-permute-start.9 = (bf16[160,1408]{1,0:T(8,128)(2,1)}, bf16[160,1408]{1,0:T(8,128)(2,1)}, u32[]{:S(2)}, u32[]{:S(2)}) collective-permute-start(bf16[160,1408]{1,0:T(8,128)(2,1)} %get-tuple-element.55.refs_1_), channel_id=1, source_target_pairs={{0,1},{1,2},{2,3},{3,0},{4,5},{5,6},{6,7},{7,4},{8,9},{9,10},{10,1... | collective-permute-start | bytes 1351688 | tf_op jit(solution)/shard_map/ppermute | solution.py:29
  52.1 2.7 %collective-permute-start.10 = (bf16[160,1280]{1,0:T(8,128)(2,1)}, bf16[160,1280]{1,0:T(8,128)(2,1)S(1)}, u32[]{:S(2)}, u32[]{:S(2)}) collective-permute-start(bf16[160,1280]{1,0:T(8,128)(2,1)} %get-tuple-element.56.refs_1_), channel_id=1, source_target_pairs={{0,12},{1,13},{2,14},{3,15},{4,0},{5,1},{6,2},{7,3},{8,4},{9,5},{1... | collective-permute-start | bytes 1228808 | tf_op jit(solution)/shard_map/ppermute | solution.py:34
  54.9 1.2 collective-permute-start.14
  56.1 4.5 %shard_map.95.first = bf16[8,20,2048]{2,1,0:T(8,128)(2,1)S(1)} custom-call(s32[2]{0:T(128)S(1)} %pad_add_fusion.1.place, bf16[160,2688]{1,0:T(8,128)(2,1)S(1)} %collective-permute-done.11.theirs, bf16[160,2688]{1,0:T(8,128)(2,1)} %get-tuple-element.65.own, bf16[1792,2048]{1,0:T(8,128)(2,1)} %down.3), custom_call_target="tpu_custom_call" | custom-call | flops 1174405120 | bytes 7340032 | tf_op jit(solution)/shard_map/pallas_call | solution.py:162
  60.6 4.0 %all-to-all-start.2 = ((bf16[4,160,512]{2,1,0:T(8,128)(2,1)}), bf16[4,160,512]{2,1,0:T(8,128)(2,1)S(1)}, u32[]{:S(2)}, u32[]{:S(2)}) async-start(bf16[4,160,512]{2,1,0:T(8,128)(2,1)} %get-tuple-element.86), calls=%async_computation.2 | async-start | bytes 1310720 | tf_op jit(solution)/shard_map/all_to_all | solution.py:42
  64.6 0.8 copy-done.6
  65.4 3.1 %collective-permute-done.9.refs_2_ = bf16[160,1408]{1,0:T(8,128)(2,1)} collective-permute-done((bf16[160,1408]{1,0:T(8,128)(2,1)}, bf16[160,1408]{1,0:T(8,128)(2,1)}, u32[]{:S(2)}, u32[]{:S(2)}) %collective-permute-start.9) | collective-permute-done | bytes 450592 | tf_op jit(solution)/shard_map/ppermute | solution.py:29
  68.5 2.7 %collective-permute-start.20 = (bf16[160,1280]{1,0:T(8,128)(2,1)}, bf16[160,1280]{1,0:T(8,128)(2,1)S(1)}, u32[]{:S(2)}, u32[]{:S(2)}) collective-permute-start(bf16[160,1280]{1,0:T(8,128)(2,1)} %copy-done.6), channel_id=1, source_target_pairs={{0,12},{1,13},{2,14},{3,15},{4,0},{5,1},{6,2},{7,3},{8,4},{9,5},{1... | collective-permute-start | bytes 1228808 | tf_op jit(solution)/shard_map/ppermute | solution.py:34
  71.2 0.7 collective-permute-start.15
  72.0 9.5 %shard_map.96 = bf16[8,20,4096]{2,1,0:T(8,128)(2,1)} custom-call(s32[2]{0:T(128)S(1)} %pad_add_fusion.1.place, bf16[8,20,2048]{2,1,0:T(8,128)(2,1)S(1)} %shard_map.95.first, bf16[160,2688]{1,0:T(8,128)(2,1)S(1)} %collective-permute-done.11.theirs, bf16[160,2688]{1,0:T(8,128)(2,1)} %get-tuple-element.65.own, bf16[2048,1792]{1,0:T(8,128)(2,1)} %gate.3, ...), custom_call_target="tpu_custom_call" | custom-call | flops 2348810240 | bytes 14680064 | tf_op jit(solution)/shard_map/pallas_call | solution.py:162
  82.1 0.9 copy-done.5
  83.1 5.0 %all-to-all-start.1 = ((bf16[8,20,4096]{2,1,0:T(8,128)(2,1)}), bf16[8,20,4096]{2,1,0:T(8,128)(2,1)S(1)}, u32[]{:S(2)}, u32[]{:S(2)}) async-start(bf16[8,20,4096]{2,1,0:T(8,128)(2,1)} %shard_map.96), calls=%async_computation.1 | async-start | bytes 3145728 | tf_op jit(solution)/shard_map/all_to_all | solution.py:491
  88.1 1.9 %collective-permute-start.22 = (bf16[4,160,512]{2,1,0:T(8,128)(2,1)}, bf16[4,160,512]{2,1,0:T(8,128)(2,1)}, u32[]{:S(2)}, u32[]{:S(2)}) collective-permute-start(bf16[4,160,512]{2,1,0:T(8,128)(2,1)} %copy-done.5), channel_id=1, source_target_pairs={{0,128},{128,0},{1,129},{129,1},{2,130},{130,2},{3,131},{131,3},{4... | collective-permute-start | bytes 1966088 | tf_op jit(solution)/shard_map/ppermute | solution.py:38
  90.2 5.4 %shard_map.97 = (f32[256,1408]{1,0:T(8,128)S(1)}, bf16[256,1408]{1,0:T(8,128)(2,1)S(1)}, bf16[256,1408]{1,0:T(8,128)(2,1)S(1)}, bf16[128,1408]{1,0:T(8,128)(2,1)S(1)}, bf16[128,1408]{1,0:T(8,128)(2,1)S(1)}) custom-call(s32[2]{0:T(128)S(1)} %pad_add_fusion.place, bf16[160,1408]{1,0:T(8,128)(2,1)S(1)} %collective-permute-done.12.refs_0_, ...), custom_call_target="tpu_custom_call" | custom-call | flops 1845493760 | bytes 4423680 | tf_op jit(solution)/shard_map/pallas_call | solution.py:162
  95.6 1.6 %collective-permute-start.16 = (bf16[128,1408]{1,0:T(8,128)(2,1)S(1)}, bf16[128,1408]{1,0:T(8,128)(2,1)S(1)}, u32[]{:S(2)}, u32[]{:S(2)}) collective-permute-start(bf16[128,1408]{1,0:T(8,128)(2,1)S(1)} %get-tuple-element.71), channel_id=1, source_target_pairs={{0,4},{1,5},{2,6},{3,7},{4,8},{5,9},{6,10},{7,11},{8,12},{9,13},{1... | collective-permute-start | bytes 1081352 | tf_op jit(solution)/shard_map/ppermute | solution.py:34
  97.2 1.2 collective-permute-start.17
  98.4 4.5 %shard_map.101 = (f32[256,1280]{1,0:T(8,128)S(1)}, bf16[256,1280]{1,0:T(8,128)(2,1)S(1)}, bf16[256,1280]{1,0:T(8,128)(2,1)S(1)}, bf16[128,1280]{1,0:T(8,128)(2,1)S(1)}, bf16[128,1280]{1,0:T(8,128)(2,1)S(1)}) custom-call(s32[2]{0:T(128)S(1)} %pad_add_fusion.2.place, bf16[160,1280]{1,0:T(8,128)(2,1)S(1)} %copy-done.3, ...), custom_call_target="tpu_custom_call" | custom-call | flops 1677721600 | bytes 2949120 | tf_op jit(solution)/shard_map/pallas_call | solution.py:162
  103.5 2.4 %collective-permute-start.24 = (bf16[128,1280]{1,0:T(8,128)(2,1)S(1)}, bf16[128,1280]{1,0:T(8,128)(2,1)S(1)}, u32[]{:S(2)}, u32[]{:S(2)}) collective-permute-start(bf16[128,1280]{1,0:T(8,128)(2,1)S(1)} %get-tuple-element.91), channel_id=1, source_target_pairs={{0,3},{1,0},{2,1},{3,2},{4,7},{5,4},{6,5},{7,6},{8,11},{9,8},{10,9... | collective-permute-start | bytes 983048 | tf_op jit(solution)/shard_map/ppermute | solution.py:29
  105.9 1.0 collective-permute-done.16.from_before
  106.9 1.3 shard_map.98
  108.7 2.1 %collective-permute-start.19 = (bf16[256,1408]{1,0:T(8,128)(2,1)}, bf16[256,1408]{1,0:T(8,128)(2,1)}, u32[]{:S(2)}, u32[]{:S(2)}) collective-permute-start(bf16[256,1408]{1,0:T(8,128)(2,1)} %get-tuple-element.74), channel_id=1, source_target_pairs={{0,12},{1,13},{2,14},{3,15},{4,0},{5,1},{6,2},{7,3},{8,4},{9,5},{1... | collective-permute-start | bytes 2162696 | tf_op jit(solution)/shard_map/ppermute | solution.py:34
  110.9 2.3 %collective-permute-done.23.from_before = bf16[128,1280]{1,0:T(8,128)(2,1)S(1)} collective-permute-done((bf16[128,1280]{1,0:T(8,128)(2,1)S(1)}, bf16[128,1280]{1,0:T(8,128)(2,1)S(1)}, u32[]{:S(2)}, u32[]{:S(2)}) %collective-permute-start.23) | collective-permute-done | bytes 327712 | tf_op jit(solution)/shard_map/ppermute | solution.py:29
  113.1 1.3 shard_map.102
  114.4 2.7 %collective-permute-start.26 = (bf16[256,1280]{1,0:T(8,128)(2,1)}, bf16[256,1280]{1,0:T(8,128)(2,1)}, u32[]{:S(2)}, u32[]{:S(2)}) collective-permute-start(bf16[256,1280]{1,0:T(8,128)(2,1)} %get-tuple-element.93), channel_id=1, source_target_pairs={{0,3},{1,0},{2,1},{3,2},{4,7},{5,4},{6,5},{7,6},{8,11},{9,8},{10,9... | collective-permute-start | bytes 1966088 | tf_op jit(solution)/shard_map/ppermute | solution.py:29
  117.1 11.5 %all-to-all-done.1.moved = bf16[8,20,4096]{2,1,0:T(8,128)(2,1)S(1)} async-done(((bf16[8,20,4096]{2,1,0:T(8,128)(2,1)}), bf16[8,20,4096]{2,1,0:T(8,128)(2,1)S(1)}, u32[]{:S(2)}, u32[]{:S(2)}) %all-to-all-start.1) | async-done | bytes 1310752 | tf_op jit(solution)/shard_map/all_to_all | solution.py:491
  128.5 0.8 shard_map.99
  129.4 1.7 %shard_map.100 = (bf16[128,1408]{1,0:T(8,128)(2,1)S(1)}, bf16[128,1408]{1,0:T(8,128)(2,1)S(1)}) custom-call(f32[256,1408]{1,0:T(8,128)S(1)} %get-tuple-element.80.own, bf16[256,1408]{1,0:T(8,128)(2,1)} %collective-permute-done.18.from_before, bf16[256,1408]{1,0:T(8,128)(2,1)} %collective-permute-done.19.from_after), custom_call_target="tpu_custom_call" | custom-call | tf_op jit(solution)/shard_map/pallas_call | solution.py:60
  131.7 1.5 %shard_map.103 = (bf16[128,1280]{1,0:T(8,128)(2,1)S(1)}, bf16[128,1280]{1,0:T(8,128)(2,1)S(1)}) custom-call(f32[256,1280]{1,0:T(8,128)S(1)} %copy-done.1, bf16[256,1280]{1,0:T(8,128)(2,1)} %collective-permute-done.25.from_before, bf16[256,1280]{1,0:T(8,128)(2,1)} %collective-permute-done.26.from_after), custom_call_target="tpu_custom_call" | custom-call | tf_op jit(solution)/shard_map/pallas_call | solution.py:60
  133.2 1.4 %collective-permute-start.27 = (bf16[128,1280]{1,0:T(8,128)(2,1)S(1)}, bf16[128,1280]{1,0:T(8,128)(2,1)S(1)}, u32[]{:S(2)}, u32[]{:S(2)}) collective-permute-start(bf16[128,1280]{1,0:T(8,128)(2,1)S(1)} %get-tuple-element.95), channel_id=1, source_target_pairs={{0,128},{128,0},{1,129},{129,1},{2,130},{130,2},{3,131},{131,3},{4... | collective-permute-start | bytes 983048 | tf_op jit(solution)/shard_map/ppermute | solution.py:38
  134.7 1.3 collective-permute-done.27.other_b
  135.9 1.3 shard_map.104
  (47 shorter events, 3.2 us)
Async XLA Ops:
  1.6 11.4 %collective-permute-start.3 = (bf16[40,2048]{1,0:T(8,128)(2,1)S(1)}, bf16[40,2048]{1,0:T(8,128)(2,1)S(1)}, u32[]{:S(2)}, u32[]{:S(2)}) collective-permute-start(bf16[40,2048]{1,0:T(8,128)(2,1)S(1)} %pad_maximum_fusion.refs_0_), channel_id=1, source_target_pairs={{0,32},{16,48},{32,64},{48,80},{64,96},{80,112},{96,0},{112,16},{1... | collective-permute-start | bytes 491528 | tf_op jit(solution)/shard_map/ppermute | solution.py:24
  5.5 11.9 %collective-permute-start.1 = (bf16[40,2048]{1,0:T(8,128)(2,1)S(1)}, bf16[40,2048]{1,0:T(8,128)(2,1)S(1)}, u32[]{:S(2)}, u32[]{:S(2)}) collective-permute-start(bf16[40,2048]{1,0:T(8,128)(2,1)S(1)} %pad_maximum_fusion.refs_0_), channel_id=1, source_target_pairs={{0,96},{16,112},{32,0},{48,16},{64,32},{80,48},{96,64},{112,80},{1... | collective-permute-start | bytes 491528 | tf_op jit(solution)/shard_map/ppermute | solution.py:24
  8.6 11.4 %collective-permute-start.7 = (bf16[40,2048]{1,0:T(8,128)(2,1)S(1)}, bf16[40,2048]{1,0:T(8,128)(2,1)S(1)}, u32[]{:S(2)}, u32[]{:S(2)}) collective-permute-start(bf16[40,2048]{1,0:T(8,128)(2,1)S(1)} %pad_maximum_fusion.refs_0_), channel_id=1, source_target_pairs={{0,16},{16,32},{32,48},{48,64},{64,80},{80,96},{96,112},{112,0},{1... | collective-permute-start | bytes 491528 | tf_op jit(solution)/shard_map/ppermute | solution.py:24
  9.4 12.3 %collective-permute-start = (bf16[40,2048]{1,0:T(8,128)(2,1)S(1)}, bf16[40,2048]{1,0:T(8,128)(2,1)S(1)}, u32[]{:S(2)}, u32[]{:S(2)}) collective-permute-start(bf16[40,2048]{1,0:T(8,128)(2,1)S(1)} %pad_maximum_fusion.refs_0_), channel_id=1, source_target_pairs={{0,112},{16,0},{32,16},{48,32},{64,48},{80,64},{96,80},{112,96},{1... | collective-permute-start | bytes 491528 | tf_op jit(solution)/shard_map/ppermute | solution.py:24
  13.0 14.2 %collective-permute-start.6 = (bf16[40,2048]{1,0:T(8,128)(2,1)S(1)}, bf16[40,2048]{1,0:T(8,128)(2,1)S(1)}, u32[]{:S(2)}, u32[]{:S(2)}) collective-permute-start(bf16[40,2048]{1,0:T(8,128)(2,1)S(1)} %collective-permute-done.3.refs_7_), channel_id=1, source_target_pairs={{0,16},{16,32},{32,48},{48,64},{64,80},{80,96},{96,112},{112,0},{1... | collective-permute-start | bytes 491528 | tf_op jit(solution)/shard_map/ppermute | solution.py:24
  17.4 9.8 %collective-permute-start.2 = (bf16[40,2048]{1,0:T(8,128)(2,1)S(1)}, bf16[40,2048]{1,0:T(8,128)(2,1)S(1)}, u32[]{:S(2)}, u32[]{:S(2)}) collective-permute-start(bf16[40,2048]{1,0:T(8,128)(2,1)S(1)} %collective-permute-done.1.refs_2_), channel_id=1, source_target_pairs={{0,112},{16,0},{32,16},{48,32},{64,48},{80,64},{96,80},{112,96},{1... | collective-permute-start | bytes 491528 | tf_op jit(solution)/shard_map/ppermute | solution.py:24
  17.5 6.5 %collective-permute-start.4 = (bf16[40,1024]{1,0:T(8,128)(2,1)S(1)}, bf16[40,1024]{1,0:T(8,128)(2,1)S(1)}, u32[]{:S(2)}, u32[]{:S(2)}) collective-permute-start(bf16[40,1024]{1,0:T(8,128)(2,1)S(1)} %slice.8), channel_id=1, source_target_pairs={{0,32},{16,48},{32,64},{48,80},{64,96},{80,112},{96,0},{112,16},{1... | collective-permute-start | bytes 245768 | tf_op jit(solution)/shard_map/ppermute | solution.py:24
  20.0 7.2 %collective-permute-start.5 = (bf16[40,1024]{1,0:T(8,128)(2,1)S(1)}, bf16[40,1024]{1,0:T(8,128)(2,1)S(1)}, u32[]{:S(2)}, u32[]{:S(2)}) collective-permute-start(bf16[40,1024]{1,0:T(8,128)(2,1)S(1)} %slice.9), channel_id=1, source_target_pairs={{0,96},{16,112},{32,0},{48,16},{64,32},{80,48},{96,64},{112,80},{1... | collective-permute-start | bytes 245768 | tf_op jit(solution)/shard_map/ppermute | solution.py:24
  34.1 12.0 %collective-permute-start.8 = (f32[160,2688]{1,0:T(8,128)}, f32[160,2688]{1,0:T(8,128)S(1)}, u32[]{:S(2)}, u32[]{:S(2)}) collective-permute-start(f32[160,2688]{1,0:T(8,128)} %get-tuple-element.54), channel_id=1, source_target_pairs={{0,128},{128,0},{1,129},{129,1},{2,130},{130,2},{3,131},{131,3},{4... | collective-permute-start | bytes 5160968 | tf_op jit(solution)/shard_map/ppermute | solution.py:38
  36.1 24.5 %all-to-all-start = ((bf16[4,160,1024]{2,1,0:T(8,128)(2,1)}), bf16[4,160,1024]{2,1,0:T(8,128)(2,1)}, u32[]{:S(2)}, u32[]{:S(2)}) async-start(bf16[4,160,1024]{2,1,0:T(8,128)(2,1)} %get-tuple-element.57), calls=%async_computation | async-start | bytes 2621440 | tf_op jit(solution)/shard_map/all_to_all | solution.py:42
  46.2 1.2 copy-start.4
  50.4 5.8 %collective-permute-start.11 = (bf16[160,2688]{1,0:T(8,128)(2,1)}, bf16[160,2688]{1,0:T(8,128)(2,1)S(1)}, u32[]{:S(2)}, u32[]{:S(2)}) collective-permute-start(bf16[160,2688]{1,0:T(8,128)(2,1)} %get-tuple-element.65.own), channel_id=1, source_target_pairs={{0,128},{128,0},{1,129},{129,1},{2,130},{130,2},{3,131},{131,3},{4... | collective-permute-start | bytes 2580488 | tf_op jit(solution)/shard_map/ppermute | solution.py:38
  50.4 18.1 %collective-permute-start.9 = (bf16[160,1408]{1,0:T(8,128)(2,1)}, bf16[160,1408]{1,0:T(8,128)(2,1)}, u32[]{:S(2)}, u32[]{:S(2)}) collective-permute-start(bf16[160,1408]{1,0:T(8,128)(2,1)} %get-tuple-element.55.refs_1_), channel_id=1, source_target_pairs={{0,1},{1,2},{2,3},{3,0},{4,5},{5,6},{6,7},{7,4},{8,9},{9,10},{10,1... | collective-permute-start | bytes 1351688 | tf_op jit(solution)/shard_map/ppermute | solution.py:29
  52.1 12.5 %collective-permute-start.10 = (bf16[160,1280]{1,0:T(8,128)(2,1)}, bf16[160,1280]{1,0:T(8,128)(2,1)S(1)}, u32[]{:S(2)}, u32[]{:S(2)}) collective-permute-start(bf16[160,1280]{1,0:T(8,128)(2,1)} %get-tuple-element.56.refs_1_), channel_id=1, source_target_pairs={{0,12},{1,13},{2,14},{3,15},{4,0},{5,1},{6,2},{7,3},{8,4},{9,5},{1... | collective-permute-start | bytes 1228808 | tf_op jit(solution)/shard_map/ppermute | solution.py:34
  54.8 17.1 %collective-permute-start.13 = (bf16[160,1280]{1,0:T(8,128)(2,1)}, bf16[160,1280]{1,0:T(8,128)(2,1)}, u32[]{:S(2)}, u32[]{:S(2)}) collective-permute-start(bf16[160,1280]{1,0:T(8,128)(2,1)} %get-tuple-element.56.refs_1_), channel_id=1, source_target_pairs={{0,4},{1,5},{2,6},{3,7},{4,8},{5,9},{6,10},{7,11},{8,12},{9,13},{1... | collective-permute-start | bytes 1228808 | tf_op jit(solution)/shard_map/ppermute | solution.py:34
  54.9 17.1 %collective-permute-start.14 = (bf16[160,1408]{1,0:T(8,128)(2,1)}, bf16[160,1408]{1,0:T(8,128)(2,1)}, u32[]{:S(2)}, u32[]{:S(2)}) collective-permute-start(bf16[160,1408]{1,0:T(8,128)(2,1)} %get-tuple-element.55.refs_1_), channel_id=1, source_target_pairs={{0,3},{1,0},{2,1},{3,2},{4,7},{5,4},{6,5},{7,6},{8,11},{9,8},{10,9... | collective-permute-start | bytes 1351688 | tf_op jit(solution)/shard_map/ppermute | solution.py:29
  60.6 21.4 %all-to-all-start.2 = ((bf16[4,160,512]{2,1,0:T(8,128)(2,1)}), bf16[4,160,512]{2,1,0:T(8,128)(2,1)S(1)}, u32[]{:S(2)}, u32[]{:S(2)}) async-start(bf16[4,160,512]{2,1,0:T(8,128)(2,1)} %get-tuple-element.86), calls=%async_computation.2 | async-start | bytes 1310720 | tf_op jit(solution)/shard_map/all_to_all | solution.py:42
  64.6 0.8 copy-start.6
  68.5 13.5 %collective-permute-start.12 = (bf16[160,1408]{1,0:T(8,128)(2,1)}, bf16[160,1408]{1,0:T(8,128)(2,1)S(1)}, u32[]{:S(2)}, u32[]{:S(2)}) collective-permute-start(bf16[160,1408]{1,0:T(8,128)(2,1)} %collective-permute-done.9.refs_2_), channel_id=1, source_target_pairs={{0,1},{1,2},{2,3},{3,0},{4,5},{5,6},{6,7},{7,4},{8,9},{9,10},{10,1... | collective-permute-start | bytes 1351688 | tf_op jit(solution)/shard_map/ppermute | solution.py:29
  68.5 13.5 %collective-permute-start.20 = (bf16[160,1280]{1,0:T(8,128)(2,1)}, bf16[160,1280]{1,0:T(8,128)(2,1)S(1)}, u32[]{:S(2)}, u32[]{:S(2)}) collective-permute-start(bf16[160,1280]{1,0:T(8,128)(2,1)} %copy-done.6), channel_id=1, source_target_pairs={{0,12},{1,13},{2,14},{3,15},{4,0},{5,1},{6,2},{7,3},{8,4},{9,5},{1... | collective-permute-start | bytes 1228808 | tf_op jit(solution)/shard_map/ppermute | solution.py:34
  71.2 19.0 %collective-permute-start.15 = (bf16[4,160,1024]{2,1,0:T(8,128)(2,1)}, bf16[4,160,1024]{2,1,0:T(8,128)(2,1)}, u32[]{:S(2)}, u32[]{:S(2)}) collective-permute-start(bf16[4,160,1024]{2,1,0:T(8,128)(2,1)} %all-to-all-done.refs_4_), channel_id=1, source_target_pairs={{0,128},{128,0},{1,129},{129,1},{2,130},{130,2},{3,131},{131,3},{4... | collective-permute-start | bytes 3932168 | tf_op jit(solution)/shard_map/ppermute | solution.py:38
  82.0 1.0 copy-start.2
  82.1 0.9 copy-start.5
  83.1 45.5 %all-to-all-start.1 = ((bf16[8,20,4096]{2,1,0:T(8,128)(2,1)}), bf16[8,20,4096]{2,1,0:T(8,128)(2,1)S(1)}, u32[]{:S(2)}, u32[]{:S(2)}) async-start(bf16[8,20,4096]{2,1,0:T(8,128)(2,1)} %shard_map.96), calls=%async_computation.1 | async-start | bytes 3145728 | tf_op jit(solution)/shard_map/all_to_all | solution.py:491
  88.1 10.3 %collective-permute-start.22 = (bf16[4,160,512]{2,1,0:T(8,128)(2,1)}, bf16[4,160,512]{2,1,0:T(8,128)(2,1)}, u32[]{:S(2)}, u32[]{:S(2)}) collective-permute-start(bf16[4,160,512]{2,1,0:T(8,128)(2,1)} %copy-done.5), channel_id=1, source_target_pairs={{0,128},{128,0},{1,129},{129,1},{2,130},{130,2},{3,131},{131,3},{4... | collective-permute-start | bytes 1966088 | tf_op jit(solution)/shard_map/ppermute | solution.py:38
  90.2 8.2 %copy-start.3 = (bf16[160,1280]{1,0:T(8,128)(2,1)S(1)}, bf16[160,1280]{1,0:T(8,128)(2,1)}, u32[]{:S(2)}) copy-start(bf16[160,1280]{1,0:T(8,128)(2,1)} %copy-done.2) | copy-start | bytes 1228804
  95.6 11.3 %collective-permute-start.16 = (bf16[128,1408]{1,0:T(8,128)(2,1)S(1)}, bf16[128,1408]{1,0:T(8,128)(2,1)S(1)}, u32[]{:S(2)}, u32[]{:S(2)}) collective-permute-start(bf16[128,1408]{1,0:T(8,128)(2,1)S(1)} %get-tuple-element.71), channel_id=1, source_target_pairs={{0,4},{1,5},{2,6},{3,7},{4,8},{5,9},{6,10},{7,11},{8,12},{9,13},{1... | collective-permute-start | bytes 1081352 | tf_op jit(solution)/shard_map/ppermute | solution.py:34
  97.2 9.7 %collective-permute-start.17 = (bf16[128,1408]{1,0:T(8,128)(2,1)S(1)}, bf16[128,1408]{1,0:T(8,128)(2,1)S(1)}, u32[]{:S(2)}, u32[]{:S(2)}) collective-permute-start(bf16[128,1408]{1,0:T(8,128)(2,1)S(1)} %get-tuple-element.72), channel_id=1, source_target_pairs={{0,12},{1,13},{2,14},{3,15},{4,0},{5,1},{6,2},{7,3},{8,4},{9,5},{1... | collective-permute-start | bytes 1081352 | tf_op jit(solution)/shard_map/ppermute | solution.py:34
  102.9 11.5 %copy-start = (f32[256,1280]{1,0:T(8,128)}, f32[256,1280]{1,0:T(8,128)S(1)}, u32[]{:S(2)}) copy-start(f32[256,1280]{1,0:T(8,128)S(1)} %get-tuple-element.87.own) | copy-start | bytes 3932164
  103.0 10.2 %collective-permute-start.23 = (bf16[128,1280]{1,0:T(8,128)(2,1)S(1)}, bf16[128,1280]{1,0:T(8,128)(2,1)S(1)}, u32[]{:S(2)}, u32[]{:S(2)}) collective-permute-start(bf16[128,1280]{1,0:T(8,128)(2,1)S(1)} %get-tuple-element.90), channel_id=1, source_target_pairs={{0,1},{1,2},{2,3},{3,0},{4,5},{5,6},{6,7},{7,4},{8,9},{9,10},{10,1... | collective-permute-start | bytes 983048 | tf_op jit(solution)/shard_map/ppermute | solution.py:29
  103.5 9.6 %collective-permute-start.24 = (bf16[128,1280]{1,0:T(8,128)(2,1)S(1)}, bf16[128,1280]{1,0:T(8,128)(2,1)S(1)}, u32[]{:S(2)}, u32[]{:S(2)}) collective-permute-start(bf16[128,1280]{1,0:T(8,128)(2,1)S(1)} %get-tuple-element.91), channel_id=1, source_target_pairs={{0,3},{1,0},{2,1},{3,2},{4,7},{5,4},{6,5},{7,6},{8,11},{9,8},{10,9... | collective-permute-start | bytes 983048 | tf_op jit(solution)/shard_map/ppermute | solution.py:29
  108.2 21.2 %collective-permute-start.18 = (bf16[256,1408]{1,0:T(8,128)(2,1)}, bf16[256,1408]{1,0:T(8,128)(2,1)}, u32[]{:S(2)}, u32[]{:S(2)}) collective-permute-start(bf16[256,1408]{1,0:T(8,128)(2,1)} %get-tuple-element.73), channel_id=1, source_target_pairs={{0,4},{1,5},{2,6},{3,7},{4,8},{5,9},{6,10},{7,11},{8,12},{9,13},{1... | collective-permute-start | bytes 2162696 | tf_op jit(solution)/shard_map/ppermute | solution.py:34
  108.7 20.7 %collective-permute-start.19 = (bf16[256,1408]{1,0:T(8,128)(2,1)}, bf16[256,1408]{1,0:T(8,128)(2,1)}, u32[]{:S(2)}, u32[]{:S(2)}) collective-permute-start(bf16[256,1408]{1,0:T(8,128)(2,1)} %get-tuple-element.74), channel_id=1, source_target_pairs={{0,12},{1,13},{2,14},{3,15},{4,0},{5,1},{6,2},{7,3},{8,4},{9,5},{1... | collective-permute-start | bytes 2162696 | tf_op jit(solution)/shard_map/ppermute | solution.py:34
  114.4 17.3 %collective-permute-start.25 = (bf16[256,1280]{1,0:T(8,128)(2,1)}, bf16[256,1280]{1,0:T(8,128)(2,1)}, u32[]{:S(2)}, u32[]{:S(2)}) collective-permute-start(bf16[256,1280]{1,0:T(8,128)(2,1)} %get-tuple-element.92), channel_id=1, source_target_pairs={{0,1},{1,2},{2,3},{3,0},{4,5},{5,6},{6,7},{7,4},{8,9},{9,10},{10,1... | collective-permute-start | bytes 1966088 | tf_op jit(solution)/shard_map/ppermute | solution.py:29
  114.4 17.3 %collective-permute-start.26 = (bf16[256,1280]{1,0:T(8,128)(2,1)}, bf16[256,1280]{1,0:T(8,128)(2,1)}, u32[]{:S(2)}, u32[]{:S(2)}) collective-permute-start(bf16[256,1280]{1,0:T(8,128)(2,1)} %get-tuple-element.93), channel_id=1, source_target_pairs={{0,3},{1,0},{2,1},{3,2},{4,7},{5,4},{6,5},{7,6},{8,11},{9,8},{10,9... | collective-permute-start | bytes 1966088 | tf_op jit(solution)/shard_map/ppermute | solution.py:29
  129.4 2.4 %copy-start.1 = (f32[256,1280]{1,0:T(8,128)S(1)}, f32[256,1280]{1,0:T(8,128)}, u32[]{:S(2)}) copy-start(f32[256,1280]{1,0:T(8,128)} %copy-done) | copy-start | bytes 3932164
  131.1 4.8 %collective-permute-start.21 = (bf16[128,1408]{1,0:T(8,128)(2,1)S(1)}, bf16[128,1408]{1,0:T(8,128)(2,1)S(1)}, u32[]{:S(2)}, u32[]{:S(2)}) collective-permute-start(bf16[128,1408]{1,0:T(8,128)(2,1)S(1)} %get-tuple-element.84), channel_id=1, source_target_pairs={{0,128},{128,0},{1,129},{129,1},{2,130},{130,2},{3,131},{131,3},{4... | collective-permute-start | bytes 1081352 | tf_op jit(solution)/shard_map/ppermute | solution.py:38
  133.2 2.7 %collective-permute-start.27 = (bf16[128,1280]{1,0:T(8,128)(2,1)S(1)}, bf16[128,1280]{1,0:T(8,128)(2,1)S(1)}, u32[]{:S(2)}, u32[]{:S(2)}) collective-permute-start(bf16[128,1280]{1,0:T(8,128)(2,1)S(1)} %get-tuple-element.95), channel_id=1, source_target_pairs={{0,128},{128,0},{1,129},{129,1},{2,130},{130,2},{3,131},{131,3},{4... | collective-permute-start | bytes 983048 | tf_op jit(solution)/shard_map/ppermute | solution.py:38
where the time goes:
time: 138 us; the launch traced here: 137 us
  starting transfers between devices  57.3 us (42%)
  Pallas kernels  47.4 us (34%)
  waiting for transfers between devices  27.4 us (20%)
  local copies, waits for them, and re-layouts  3.02 us (2%)
    pallas_call x6, Pallas kernels, in_hbm(): pl.pallas_call(kernel, in_specs=[pl.BlockSpec(memory_space=pltpu.SMEM)] +...  36.6 us
    ppermute x8, starting transfers between devices, to_z(): lax.ppermute(value, 'col', [(k, (k + step) % COLS) for k in range(COLS)])  17.8 us
    all_to_all x1, waiting for transfers between devices, body(): moved = lax.all_to_all(part, 'col', split_axis=0, concat_axis=0, tiled=True)  11.5 us
    ppermute x7, starting transfers between devices, to_y(): lax.ppermute(value, 'depth', [(k, (k + SIDE * step) % side) for k in rang...  10.9 us
    pallas_call x6, Pallas kernels, call(): pl.pallas_call(kernel, out_shape=outs, scratch_shapes=list(scratch), comp...  9.52 us
    ppermute x7, starting transfers between devices, to_x(): return lax.ppermute(value, 'depth', pairs)  8.58 us
    all_to_all x2, starting transfers between devices, swap(): lax.all_to_all(value, 'depth', split_axis=0, concat_axis=0, axis_index_gr...  8.25 us
    ppermute x8, waiting for transfers between devices, to_z(): lax.ppermute(value, 'col', [(k, (k + step) % COLS) for k in range(COLS)])  7.75 us
  transfers between devices with their start and end apart: 31, of which 10 were waited for; matrix products, arithmetic and copies ran while one was open for 0% of the time, Pallas kernels for 29%

commit v1 on v0

--- a/solution.py
+++ b/solution.py
@@ -371,8 +371,8 @@
         + [shape(2 * LANES, wide)] * 2
         + [shape(LANES, wide)] * 2,
         place,
-        pieces[3:],
-        (*pieces[:3], *columns),
+        () if cut else pieces[3:],
+        (*(pieces[3:] if cut else ()), *pieces[:3], *columns),
         [((tokens, wide), BF), ((2, *columns[0].shape), BF)],
         SIDE + 2,
         (16 * tokens * LANES * wide, 2 * tokens * (wide + 2 * width)),
@@ -457,7 +457,7 @@
     rows, model = tokens.shape
     group = rows * COLS
     half = gate_weight.shape[1] // 2
-    cut = (half // LANES // 2 + 1) * LANES
+    cut = (half // LANES // 2 + 2) * LANES
 
     blocks = gather_col(jnp.concatenate([tokens, cotangent], axis=0))
     weights = (gate_weight, up_weight, down_weight)
@@ -467,7 +467,7 @@
         swiglu_kernel,
         [pltpu.HBM((group, n), BF) for n in (half + cut, 2 * half - cut, 3 * half)],
         kept,
-        *hbm(to_core(sent)),
+        to_core(sent),
     )
     columns_a = swap(send_a, ALONG_X)
 

time: 138 us -> 144 us (1.043)
  waiting for transfers between devices: 27.4 us -> 38.1 us
  local copies, waits for them, and re-layouts: 3.02 us -> 0.03 us
    ppermute x7, waiting for transfers between devices: 1.53 us -> 6.51 us  [to_y(): lax.ppermute(value, 'depth', [(k, (k + SIDE * step) % side) for k in rang...]
    ppermute x7, waiting for transfers between devices: 5.44 us -> 9.73 us  [to_x(): return lax.ppermute(value, 'depth', pairs)]
    unnamed x14 -> x10, local copies, waits for them, and re-layouts: 3 us -> 0.02 us
  transfers between devices with their start and end apart: 31 -> 31, of which waited for: 10 -> 12; matrix products, arithmetic and copies ran while one was open for 0% -> 0% of each run, Pallas kernels for 29% -> 27%
where the time goes in v1:
time: 144 us
  starting transfers between devices  57.4 us (40%)
  Pallas kernels  46.4 us (32%)
  waiting for transfers between devices  38.1 us (26%)
    pallas_call x6, Pallas kernels, in_hbm(): pl.pallas_call(kernel, in_specs=[pl.BlockSpec(memory_space=pltpu.SMEM)] +...  37 us
    ppermute x8, starting transfers between devices, to_z(): lax.ppermute(value, 'col', [(k, (k + step) % COLS) for k in range(COLS)])  17.8 us
    all_to_all x1, waiting for transfers between devices, body(): moved = lax.all_to_all(part, 'col', split_axis=0, concat_axis=0, tiled=True)  12 us
    ppermute x7, starting transfers between devices, to_y(): lax.ppermute(value, 'depth', [(k, (k + SIDE * step) % side) for k in rang...  11.1 us
    ppermute x7, waiting for transfers between devices, to_x(): return lax.ppermute(value, 'depth', pairs)  9.73 us
    all_to_all x2, starting transfers between devices, swap(): lax.all_to_all(value, 'depth', split_axis=0, concat_axis=0, axis_index_gr...  8.48 us
    ppermute x7, starting transfers between devices, to_x(): return lax.ppermute(value, 'depth', pairs)  8.43 us
    pallas_call x6, Pallas kernels, call(): pl.pallas_call(kernel, out_shape=outs, scratch_shapes=list(scratch), comp...  8.09 us
  transfers between devices with their start and end apart: 31, of which 12 were waited for; matrix products, arithmetic and copies ran while one was open for 0% of the time, Pallas kernels for 27%

profile of v1, /device:TPU:1, one launch (start us, length us, event | category | flops | bytes accessed | tf_op | source)
XLA Modules:
  0.0 143.9 jit_solution(6264447149799432492)
XLA Ops:
  0.6 1.0 pad_maximum_fusion.refs_0_
  1.6 3.9 %collective-permute-start.3 = (bf16[40,2048]{1,0:T(8,128)(2,1)S(1)}, bf16[40,2048]{1,0:T(8,128)(2,1)S(1)}, u32[]{:S(2)}, u32[]{:S(2)}) collective-permute-start(bf16[40,2048]{1,0:T(8,128)(2,1)S(1)} %pad_maximum_fusion.refs_0_), channel_id=1, source_target_pairs={{0,32},{16,48},{32,64},{48,80},{64,96},{80,112},{96,0},{112,16},{1... | collective-permute-start | bytes 491528 | tf_op jit(solution)/shard_map/ppermute | solution.py:24
  5.5 3.1 %collective-permute-start.1 = (bf16[40,2048]{1,0:T(8,128)(2,1)S(1)}, bf16[40,2048]{1,0:T(8,128)(2,1)S(1)}, u32[]{:S(2)}, u32[]{:S(2)}) collective-permute-start(bf16[40,2048]{1,0:T(8,128)(2,1)S(1)} %pad_maximum_fusion.refs_0_), channel_id=1, source_target_pairs={{0,96},{16,112},{32,0},{48,16},{64,32},{80,48},{96,64},{112,80},{1... | collective-permute-start | bytes 491528 | tf_op jit(solution)/shard_map/ppermute | solution.py:24
  8.6 0.7 collective-permute-start.7
  9.4 1.9 %collective-permute-start = (bf16[40,2048]{1,0:T(8,128)(2,1)S(1)}, bf16[40,2048]{1,0:T(8,128)(2,1)S(1)}, u32[]{:S(2)}, u32[]{:S(2)}) collective-permute-start(bf16[40,2048]{1,0:T(8,128)(2,1)S(1)} %pad_maximum_fusion.refs_0_), channel_id=1, source_target_pairs={{0,112},{16,0},{32,16},{48,32},{64,48},{80,64},{96,80},{112,96},{1... | collective-permute-start | bytes 491528 | tf_op jit(solution)/shard_map/ppermute | solution.py:24
  11.3 1.7 %collective-permute-done.3.refs_7_ = bf16[40,2048]{1,0:T(8,128)(2,1)S(1)} collective-permute-done((bf16[40,2048]{1,0:T(8,128)(2,1)S(1)}, bf16[40,2048]{1,0:T(8,128)(2,1)S(1)}, u32[]{:S(2)}, u32[]{:S(2)}) %collective-permute-start.3) | collective-permute-done | bytes 163872 | tf_op jit(solution)/shard_map/ppermute | solution.py:24
  13.0 3.9 %collective-permute-start.6 = (bf16[40,2048]{1,0:T(8,128)(2,1)S(1)}, bf16[40,2048]{1,0:T(8,128)(2,1)S(1)}, u32[]{:S(2)}, u32[]{:S(2)}) collective-permute-start(bf16[40,2048]{1,0:T(8,128)(2,1)S(1)} %collective-permute-done.3.refs_7_), channel_id=1, source_target_pairs={{0,16},{16,32},{32,48},{48,64},{64,80},{80,96},{96,112},{112,0},{1... | collective-permute-start | bytes 491528 | tf_op jit(solution)/shard_map/ppermute | solution.py:24
  17.5 2.6 %collective-permute-start.4 = (bf16[40,1024]{1,0:T(8,128)(2,1)S(1)}, bf16[40,1024]{1,0:T(8,128)(2,1)S(1)}, u32[]{:S(2)}, u32[]{:S(2)}) collective-permute-start(bf16[40,1024]{1,0:T(8,128)(2,1)S(1)} %slice.8), channel_id=1, source_target_pairs={{0,32},{16,48},{32,64},{48,80},{64,96},{80,112},{96,0},{112,16},{1... | collective-permute-start | bytes 245768 | tf_op jit(solution)/shard_map/ppermute | solution.py:24
  20.0 1.6 %collective-permute-start.5 = (bf16[40,1024]{1,0:T(8,128)(2,1)S(1)}, bf16[40,1024]{1,0:T(8,128)(2,1)S(1)}, u32[]{:S(2)}, u32[]{:S(2)}) collective-permute-start(bf16[40,1024]{1,0:T(8,128)(2,1)S(1)} %slice.9), channel_id=1, source_target_pairs={{0,96},{16,112},{32,0},{48,16},{64,32},{80,48},{96,64},{112,80},{1... | collective-permute-start | bytes 245768 | tf_op jit(solution)/shard_map/ppermute | solution.py:24
  21.7 2.3 %collective-permute-done.4.refs_4_ = bf16[40,1024]{1,0:T(8,128)(2,1)S(1)} collective-permute-done((bf16[40,1024]{1,0:T(8,128)(2,1)S(1)}, bf16[40,1024]{1,0:T(8,128)(2,1)S(1)}, u32[]{:S(2)}, u32[]{:S(2)}) %collective-permute-start.4) | collective-permute-done | bytes 81952 | tf_op jit(solution)/shard_map/ppermute | solution.py:24
  24.0 3.2 %collective-permute-done.5.refs_5_ = bf16[40,1024]{1,0:T(8,128)(2,1)S(1)} collective-permute-done((bf16[40,1024]{1,0:T(8,128)(2,1)S(1)}, bf16[40,1024]{1,0:T(8,128)(2,1)S(1)}, u32[]{:S(2)}, u32[]{:S(2)}) %collective-permute-start.5) | collective-permute-done | bytes 81952 | tf_op jit(solution)/shard_map/ppermute | solution.py:24
  27.2 6.9 %shard_map.92 = (f32[160,2688]{1,0:T(8,128)}, bf16[160,2048]{1,0:T(8,128)(2,1)S(1)}, bf16[160,2048]{1,0:T(8,128)(2,1)S(1)}, bf16[4,160,1024]{2,1,0:T(8,128)(2,1)}, bf16[4,160,512]{2,1,0:T(8,128)(2,1)}) custom-call(s32[1]{0:T(128)} %bitcast.3.which, bf16[40,2048]{1,0:T(8,128)(2,1)S(1)} %pad_maximum_fusion.refs_0_, ...), custom_call_target="tpu_custom_call" | custom-call | tf_op jit(solution)/shard_map/pallas_call | solution.py:162
  34.1 2.0 %collective-permute-start.8 = (f32[160,2688]{1,0:T(8,128)}, f32[160,2688]{1,0:T(8,128)S(1)}, u32[]{:S(2)}, u32[]{:S(2)}) collective-permute-start(f32[160,2688]{1,0:T(8,128)} %get-tuple-element.54), channel_id=1, source_target_pairs={{0,128},{128,0},{1,129},{129,1},{2,130},{130,2},{3,131},{131,3},{4... | collective-permute-start | bytes 5160968 | tf_op jit(solution)/shard_map/ppermute | solution.py:38
  36.1 4.3 %all-to-all-start = ((bf16[4,160,1024]{2,1,0:T(8,128)(2,1)}), bf16[4,160,1024]{2,1,0:T(8,128)(2,1)}, u32[]{:S(2)}, u32[]{:S(2)}) async-start(bf16[4,160,1024]{2,1,0:T(8,128)(2,1)} %get-tuple-element.57), calls=%async_computation | async-start | bytes 2621440 | tf_op jit(solution)/shard_map/all_to_all | solution.py:42
  40.4 5.7 %shard_map.93.own = f32[160,2688]{1,0:T(8,128)S(1)} custom-call(s32[1]{0:T(128)} %bitcast.2.which, bf16[160,2048]{1,0:T(8,128)(2,1)S(1)} %get-tuple-element.52.feat, bf16[160,2048]{1,0:T(8,128)(2,1)S(1)} %get-tuple-element.53.upst, bf16[2048,1792]{1,0:T(8,128)(2,1)} %gate.3, bf16[2048,1792]{1,0:T(8,128)(2,1)} %up.3, bf16[1792,2048]{1,0:T(8,128)(2,1)} %down.3), custom_call_target="tpu_custom_call" | custom-call | tf_op jit(solution)/shard_map/pallas_call | solution.py:162
  46.2 1.6 %shard_map.94 = (bf16[160,1536]{1,0:T(8,128)(2,1)}, bf16[160,1152]{1,0:T(8,128)(2,1)}, bf16[160,2688]{1,0:T(8,128)(2,1)}) custom-call(f32[160,2688]{1,0:T(8,128)S(1)} %shard_map.93.own, f32[160,2688]{1,0:T(8,128)S(1)} %collective-permute-done.8.theirs), custom_call_target="tpu_custom_call" | custom-call | tf_op jit(solution)/shard_map/pallas_call | solution.py:60
  47.8 1.7 %collective-permute-start.9 = (bf16[160,1536]{1,0:T(8,128)(2,1)}, bf16[160,1536]{1,0:T(8,128)(2,1)S(1)}, u32[]{:S(2)}, u32[]{:S(2)}) collective-permute-start(bf16[160,1536]{1,0:T(8,128)(2,1)} %get-tuple-element.55.refs_1_), channel_id=1, source_target_pairs={{0,1},{1,2},{2,3},{3,0},{4,5},{5,6},{6,7},{7,4},{8,9},{9,10},{10,1... | collective-permute-start | bytes 1474568 | tf_op jit(solution)/shard_map/ppermute | solution.py:29
  49.5 2.7 %collective-permute-start.10 = (bf16[160,1152]{1,0:T(8,128)(2,1)}, bf16[160,1152]{1,0:T(8,128)(2,1)S(1)}, u32[]{:S(2)}, u32[]{:S(2)}) collective-permute-start(bf16[160,1152]{1,0:T(8,128)(2,1)} %get-tuple-element.56.refs_1_), channel_id=1, source_target_pairs={{0,12},{1,13},{2,14},{3,15},{4,0},{5,1},{6,2},{7,3},{8,4},{9,5},{1... | collective-permute-start | bytes 1105928 | tf_op jit(solution)/shard_map/ppermute | solution.py:34
  52.2 1.2 collective-permute-start.14
  53.5 4.5 %shard_map.95.first = bf16[8,20,2048]{2,1,0:T(8,128)(2,1)S(1)} custom-call(s32[2]{0:T(128)S(1)} %pad_add_fusion.1.place, bf16[160,2688]{1,0:T(8,128)(2,1)S(1)} %collective-permute-done.11.theirs, bf16[160,2688]{1,0:T(8,128)(2,1)} %get-tuple-element.65.own, bf16[1792,2048]{1,0:T(8,128)(2,1)} %down.3), custom_call_target="tpu_custom_call" | custom-call | flops 1174405120 | bytes 7340032 | tf_op jit(solution)/shard_map/pallas_call | solution.py:162
  58.6 1.5 %collective-permute-done.10.refs_3_ = bf16[160,1152]{1,0:T(8,128)(2,1)S(1)} collective-permute-done((bf16[160,1152]{1,0:T(8,128)(2,1)}, bf16[160,1152]{1,0:T(8,128)(2,1)S(1)}, u32[]{:S(2)}, u32[]{:S(2)}) %collective-permute-start.10) | collective-permute-done | bytes 368672 | tf_op jit(solution)/shard_map/ppermute | solution.py:34
  60.0 9.1 %collective-permute-done.9.refs_2_ = bf16[160,1536]{1,0:T(8,128)(2,1)S(1)} collective-permute-done((bf16[160,1536]{1,0:T(8,128)(2,1)}, bf16[160,1536]{1,0:T(8,128)(2,1)S(1)}, u32[]{:S(2)}, u32[]{:S(2)}) %collective-permute-start.9) | collective-permute-done | bytes 491552 | tf_op jit(solution)/shard_map/ppermute | solution.py:29
  69.2 4.2 %all-to-all-start.2 = ((bf16[4,160,512]{2,1,0:T(8,128)(2,1)}), bf16[4,160,512]{2,1,0:T(8,128)(2,1)}, u32[]{:S(2)}, u32[]{:S(2)}) async-start(bf16[4,160,512]{2,1,0:T(8,128)(2,1)} %get-tuple-element.86), calls=%async_computation.2 | async-start | bytes 1310720 | tf_op jit(solution)/shard_map/all_to_all | solution.py:42
  73.4 0.8 collective-permute-start.15
  74.2 3.0 %collective-permute-start.20 = (bf16[160,1152]{1,0:T(8,128)(2,1)}, bf16[160,1152]{1,0:T(8,128)(2,1)S(1)}, u32[]{:S(2)}, u32[]{:S(2)}) collective-permute-start(bf16[160,1152]{1,0:T(8,128)(2,1)} %copy-done.4), channel_id=1, source_target_pairs={{0,12},{1,13},{2,14},{3,15},{4,0},{5,1},{6,2},{7,3},{8,4},{9,5},{1... | collective-permute-start | bytes 1105928 | tf_op jit(solution)/shard_map/ppermute | solution.py:34
  77.2 9.5 %shard_map.96 = bf16[8,20,4096]{2,1,0:T(8,128)(2,1)} custom-call(s32[2]{0:T(128)S(1)} %pad_add_fusion.1.place, bf16[8,20,2048]{2,1,0:T(8,128)(2,1)S(1)} %shard_map.95.first, bf16[160,2688]{1,0:T(8,128)(2,1)S(1)} %collective-permute-done.11.theirs, bf16[160,2688]{1,0:T(8,128)(2,1)} %get-tuple-element.65.own, bf16[2048,1792]{1,0:T(8,128)(2,1)} %gate.3, ...), custom_call_target="tpu_custom_call" | custom-call | flops 2348810240 | bytes 14680064 | tf_op jit(solution)/shard_map/pallas_call | solution.py:162
  86.7 3.2 %collective-permute-done.20.refs_0_ = bf16[160,1152]{1,0:T(8,128)(2,1)S(1)} collective-permute-done((bf16[160,1152]{1,0:T(8,128)(2,1)}, bf16[160,1152]{1,0:T(8,128)(2,1)S(1)}, u32[]{:S(2)}, u32[]{:S(2)}) %collective-permute-start.20) | collective-permute-done | bytes 368672 | tf_op jit(solution)/shard_map/ppermute | solution.py:34
  89.9 5.0 %all-to-all-start.1 = ((bf16[8,20,4096]{2,1,0:T(8,128)(2,1)}), bf16[8,20,4096]{2,1,0:T(8,128)(2,1)S(1)}, u32[]{:S(2)}, u32[]{:S(2)}) async-start(bf16[8,20,4096]{2,1,0:T(8,128)(2,1)} %shard_map.96), calls=%async_computation.1 | async-start | bytes 3145728 | tf_op jit(solution)/shard_map/all_to_all | solution.py:491
  94.9 2.0 %collective-permute-start.22 = (bf16[4,160,512]{2,1,0:T(8,128)(2,1)}, bf16[4,160,512]{2,1,0:T(8,128)(2,1)}, u32[]{:S(2)}, u32[]{:S(2)}) collective-permute-start(bf16[4,160,512]{2,1,0:T(8,128)(2,1)} %all-to-all-done.2.refs_4_), channel_id=1, source_target_pairs={{0,128},{128,0},{1,129},{129,1},{2,130},{130,2},{3,131},{131,3},{4... | collective-permute-start | bytes 1966088 | tf_op jit(solution)/shard_map/ppermute | solution.py:38
  97.0 5.9 %shard_map.97 = (f32[256,1536]{1,0:T(8,128)S(1)}, bf16[256,1536]{1,0:T(8,128)(2,1)S(1)}, bf16[256,1536]{1,0:T(8,128)(2,1)S(1)}, bf16[128,1536]{1,0:T(8,128)(2,1)S(1)}, bf16[128,1536]{1,0:T(8,128)(2,1)S(1)}) custom-call(s32[2]{0:T(128)S(1)} %pad_add_fusion.place, bf16[160,1536]{1,0:T(8,128)(2,1)} %collective-permute-done.12.refs_0_, ...), custom_call_target="tpu_custom_call" | custom-call | flops 2013265920 | bytes 4587520 | tf_op jit(solution)/shard_map/pallas_call | solution.py:162
  102.8 1.3 collective-permute-start.16
  104.1 1.5 %collective-permute-start.17 = (bf16[128,1536]{1,0:T(8,128)(2,1)S(1)}, bf16[128,1536]{1,0:T(8,128)(2,1)S(1)}, u32[]{:S(2)}, u32[]{:S(2)}) collective-permute-start(bf16[128,1536]{1,0:T(8,128)(2,1)S(1)} %get-tuple-element.72), channel_id=1, source_target_pairs={{0,12},{1,13},{2,14},{3,15},{4,0},{5,1},{6,2},{7,3},{8,4},{9,5},{1... | collective-permute-start | bytes 1179656 | tf_op jit(solution)/shard_map/ppermute | solution.py:34
  105.7 4.4 %shard_map.101 = (f32[256,1152]{1,0:T(8,128)S(1)}, bf16[256,1152]{1,0:T(8,128)(2,1)S(1)}, bf16[256,1152]{1,0:T(8,128)(2,1)S(1)}, bf16[128,1152]{1,0:T(8,128)(2,1)S(1)}, bf16[128,1152]{1,0:T(8,128)(2,1)S(1)}) custom-call(s32[2]{0:T(128)S(1)} %pad_add_fusion.2.place, bf16[160,1152]{1,0:T(8,128)(2,1)S(1)} %collective-permute-done.20.refs_0_, ...), custom_call_target="tpu_custom_call" | custom-call | flops 1509949440 | bytes 2785280 | tf_op jit(solution)/shard_map/pallas_call | solution.py:162
  110.3 2.7 %collective-permute-start.24 = (bf16[128,1152]{1,0:T(8,128)(2,1)S(1)}, bf16[128,1152]{1,0:T(8,128)(2,1)S(1)}, u32[]{:S(2)}, u32[]{:S(2)}) collective-permute-start(bf16[128,1152]{1,0:T(8,128)(2,1)S(1)} %get-tuple-element.91), channel_id=1, source_target_pairs={{0,3},{1,0},{2,1},{3,2},{4,7},{5,4},{6,5},{7,6},{8,11},{9,8},{10,9... | collective-permute-start | bytes 884744 | tf_op jit(solution)/shard_map/ppermute | solution.py:29
  113.0 1.9 %collective-permute-done.16.from_before = bf16[128,1536]{1,0:T(8,128)(2,1)S(1)} collective-permute-done((bf16[128,1536]{1,0:T(8,128)(2,1)S(1)}, bf16[128,1536]{1,0:T(8,128)(2,1)S(1)}, u32[]{:S(2)}, u32[]{:S(2)}) %collective-permute-start.16) | collective-permute-done | bytes 393248 | tf_op jit(solution)/shard_map/ppermute | solution.py:34
  114.9 1.3 shard_map.98
  116.7 2.1 %collective-permute-start.19 = (bf16[256,1536]{1,0:T(8,128)(2,1)}, bf16[256,1536]{1,0:T(8,128)(2,1)}, u32[]{:S(2)}, u32[]{:S(2)}) collective-permute-start(bf16[256,1536]{1,0:T(8,128)(2,1)} %get-tuple-element.74), channel_id=1, source_target_pairs={{0,12},{1,13},{2,14},{3,15},{4,0},{5,1},{6,2},{7,3},{8,4},{9,5},{1... | collective-permute-start | bytes 2359304 | tf_op jit(solution)/shard_map/ppermute | solution.py:34
  118.8 0.6 collective-permute-done.23.from_before
  119.4 1.2 shard_map.102
  120.6 0.9 collective-permute-start.25
  121.5 1.8 %collective-permute-start.26 = (bf16[256,1152]{1,0:T(8,128)(2,1)}, bf16[256,1152]{1,0:T(8,128)(2,1)}, u32[]{:S(2)}, u32[]{:S(2)}) collective-permute-start(bf16[256,1152]{1,0:T(8,128)(2,1)} %get-tuple-element.93), channel_id=1, source_target_pairs={{0,3},{1,0},{2,1},{3,2},{4,7},{5,4},{6,5},{7,6},{8,11},{9,8},{10,9... | collective-permute-start | bytes 1769480 | tf_op jit(solution)/shard_map/ppermute | solution.py:29
  123.3 12.0 %all-to-all-done.1.moved = bf16[8,20,4096]{2,1,0:T(8,128)(2,1)S(1)} async-done(((bf16[8,20,4096]{2,1,0:T(8,128)(2,1)}), bf16[8,20,4096]{2,1,0:T(8,128)(2,1)S(1)}, u32[]{:S(2)}, u32[]{:S(2)}) %all-to-all-start.1) | async-done | bytes 1310752 | tf_op jit(solution)/shard_map/all_to_all | solution.py:491
  135.3 0.8 shard_map.99
  136.2 1.8 %shard_map.100 = (bf16[128,1536]{1,0:T(8,128)(2,1)S(1)}, bf16[128,1536]{1,0:T(8,128)(2,1)S(1)}) custom-call(f32[256,1536]{1,0:T(8,128)S(1)} %get-tuple-element.80.own, bf16[256,1536]{1,0:T(8,128)(2,1)} %collective-permute-done.18.from_before, bf16[256,1536]{1,0:T(8,128)(2,1)} %collective-permute-done.19.from_after), custom_call_target="tpu_custom_call" | custom-call | tf_op jit(solution)/shard_map/pallas_call | solution.py:60
  137.9 1.5 %collective-permute-start.21 = (bf16[128,1536]{1,0:T(8,128)(2,1)S(1)}, bf16[128,1536]{1,0:T(8,128)(2,1)S(1)}, u32[]{:S(2)}, u32[]{:S(2)}) collective-permute-start(bf16[128,1536]{1,0:T(8,128)(2,1)S(1)} %get-tuple-element.84), channel_id=1, source_target_pairs={{0,128},{128,0},{1,129},{129,1},{2,130},{130,2},{3,131},{131,3},{4... | collective-permute-start | bytes 1179656 | tf_op jit(solution)/shard_map/ppermute | solution.py:38
  139.5 1.4 shard_map.103
  141.0 1.5 %collective-permute-done.27.other_b = bf16[128,1152]{1,0:T(8,128)(2,1)S(1)} collective-permute-done((bf16[128,1152]{1,0:T(8,128)(2,1)S(1)}, bf16[128,1152]{1,0:T(8,128)(2,1)S(1)}, u32[]{:S(2)}, u32[]{:S(2)}) %collective-permute-start.27) | collective-permute-done | bytes 294944 | tf_op jit(solution)/shard_map/ppermute | solution.py:38
  142.6 1.3 shard_map.104
  (43 shorter events, 2.2 us)
Async XLA Ops:
  1.6 11.4 %collective-permute-start.3 = (bf16[40,2048]{1,0:T(8,128)(2,1)S(1)}, bf16[40,2048]{1,0:T(8,128)(2,1)S(1)}, u32[]{:S(2)}, u32[]{:S(2)}) collective-permute-start(bf16[40,2048]{1,0:T(8,128)(2,1)S(1)} %pad_maximum_fusion.refs_0_), channel_id=1, source_target_pairs={{0,32},{16,48},{32,64},{48,80},{64,96},{80,112},{96,0},{112,16},{1... | collective-permute-start | bytes 491528 | tf_op jit(solution)/shard_map/ppermute | solution.py:24
  5.5 11.9 %collective-permute-start.1 = (bf16[40,2048]{1,0:T(8,128)(2,1)S(1)}, bf16[40,2048]{1,0:T(8,128)(2,1)S(1)}, u32[]{:S(2)}, u32[]{:S(2)}) collective-permute-start(bf16[40,2048]{1,0:T(8,128)(2,1)S(1)} %pad_maximum_fusion.refs_0_), channel_id=1, source_target_pairs={{0,96},{16,112},{32,0},{48,16},{64,32},{80,48},{96,64},{112,80},{1... | collective-permute-start | bytes 491528 | tf_op jit(solution)/shard_map/ppermute | solution.py:24
  8.6 11.4 %collective-permute-start.7 = (bf16[40,2048]{1,0:T(8,128)(2,1)S(1)}, bf16[40,2048]{1,0:T(8,128)(2,1)S(1)}, u32[]{:S(2)}, u32[]{:S(2)}) collective-permute-start(bf16[40,2048]{1,0:T(8,128)(2,1)S(1)} %pad_maximum_fusion.refs_0_), channel_id=1, source_target_pairs={{0,16},{16,32},{32,48},{48,64},{64,80},{80,96},{96,112},{112,0},{1... | collective-permute-start | bytes 491528 | tf_op jit(solution)/shard_map/ppermute | solution.py:24
  9.4 12.3 %collective-permute-start = (bf16[40,2048]{1,0:T(8,128)(2,1)S(1)}, bf16[40,2048]{1,0:T(8,128)(2,1)S(1)}, u32[]{:S(2)}, u32[]{:S(2)}) collective-permute-start(bf16[40,2048]{1,0:T(8,128)(2,1)S(1)} %pad_maximum_fusion.refs_0_), channel_id=1, source_target_pairs={{0,112},{16,0},{32,16},{48,32},{64,48},{80,64},{96,80},{112,96},{1... | collective-permute-start | bytes 491528 | tf_op jit(solution)/shard_map/ppermute | solution.py:24
  13.0 14.2 %collective-permute-start.6 = (bf16[40,2048]{1,0:T(8,128)(2,1)S(1)}, bf16[40,2048]{1,0:T(8,128)(2,1)S(1)}, u32[]{:S(2)}, u32[]{:S(2)}) collective-permute-start(bf16[40,2048]{1,0:T(8,128)(2,1)S(1)} %collective-permute-done.3.refs_7_), channel_id=1, source_target_pairs={{0,16},{16,32},{32,48},{48,64},{64,80},{80,96},{96,112},{112,0},{1... | collective-permute-start | bytes 491528 | tf_op jit(solution)/shard_map/ppermute | solution.py:24
  17.4 9.8 %collective-permute-start.2 = (bf16[40,2048]{1,0:T(8,128)(2,1)S(1)}, bf16[40,2048]{1,0:T(8,128)(2,1)S(1)}, u32[]{:S(2)}, u32[]{:S(2)}) collective-permute-start(bf16[40,2048]{1,0:T(8,128)(2,1)S(1)} %collective-permute-done.1.refs_2_), channel_id=1, source_target_pairs={{0,112},{16,0},{32,16},{48,32},{64,48},{80,64},{96,80},{112,96},{1... | collective-permute-start | bytes 491528 | tf_op jit(solution)/shard_map/ppermute | solution.py:24
  17.5 6.5 %collective-permute-start.4 = (bf16[40,1024]{1,0:T(8,128)(2,1)S(1)}, bf16[40,1024]{1,0:T(8,128)(2,1)S(1)}, u32[]{:S(2)}, u32[]{:S(2)}) collective-permute-start(bf16[40,1024]{1,0:T(8,128)(2,1)S(1)} %slice.8), channel_id=1, source_target_pairs={{0,32},{16,48},{32,64},{48,80},{64,96},{80,112},{96,0},{112,16},{1... | collective-permute-start | bytes 245768 | tf_op jit(solution)/shard_map/ppermute | solution.py:24
  20.0 7.2 %collective-permute-start.5 = (bf16[40,1024]{1,0:T(8,128)(2,1)S(1)}, bf16[40,1024]{1,0:T(8,128)(2,1)S(1)}, u32[]{:S(2)}, u32[]{:S(2)}) collective-permute-start(bf16[40,1024]{1,0:T(8,128)(2,1)S(1)} %slice.9), channel_id=1, source_target_pairs={{0,96},{16,112},{32,0},{48,16},{64,32},{80,48},{96,64},{112,80},{1... | collective-permute-start | bytes 245768 | tf_op jit(solution)/shard_map/ppermute | solution.py:24
  34.1 12.0 %collective-permute-start.8 = (f32[160,2688]{1,0:T(8,128)}, f32[160,2688]{1,0:T(8,128)S(1)}, u32[]{:S(2)}, u32[]{:S(2)}) collective-permute-start(f32[160,2688]{1,0:T(8,128)} %get-tuple-element.54), channel_id=1, source_target_pairs={{0,128},{128,0},{1,129},{129,1},{2,130},{130,2},{3,131},{131,3},{4... | collective-permute-start | bytes 5160968 | tf_op jit(solution)/shard_map/ppermute | solution.py:38
  36.1 22.5 %all-to-all-start = ((bf16[4,160,1024]{2,1,0:T(8,128)(2,1)}), bf16[4,160,1024]{2,1,0:T(8,128)(2,1)}, u32[]{:S(2)}, u32[]{:S(2)}) async-start(bf16[4,160,1024]{2,1,0:T(8,128)(2,1)} %get-tuple-element.57), calls=%async_computation | async-start | bytes 2621440 | tf_op jit(solution)/shard_map/all_to_all | solution.py:42
  47.8 5.8 %collective-permute-start.11 = (bf16[160,2688]{1,0:T(8,128)(2,1)}, bf16[160,2688]{1,0:T(8,128)(2,1)S(1)}, u32[]{:S(2)}, u32[]{:S(2)}) collective-permute-start(bf16[160,2688]{1,0:T(8,128)(2,1)} %get-tuple-element.65.own), channel_id=1, source_target_pairs={{0,128},{128,0},{1,129},{129,1},{2,130},{130,2},{3,131},{131,3},{4... | collective-permute-start | bytes 2580488 | tf_op jit(solution)/shard_map/ppermute | solution.py:38
  47.8 21.4 %collective-permute-start.9 = (bf16[160,1536]{1,0:T(8,128)(2,1)}, bf16[160,1536]{1,0:T(8,128)(2,1)S(1)}, u32[]{:S(2)}, u32[]{:S(2)}) collective-permute-start(bf16[160,1536]{1,0:T(8,128)(2,1)} %get-tuple-element.55.refs_1_), channel_id=1, source_target_pairs={{0,1},{1,2},{2,3},{3,0},{4,5},{5,6},{6,7},{7,4},{8,9},{9,10},{10,1... | collective-permute-start | bytes 1474568 | tf_op jit(solution)/shard_map/ppermute | solution.py:29
  49.5 10.6 %collective-permute-start.10 = (bf16[160,1152]{1,0:T(8,128)(2,1)}, bf16[160,1152]{1,0:T(8,128)(2,1)S(1)}, u32[]{:S(2)}, u32[]{:S(2)}) collective-permute-start(bf16[160,1152]{1,0:T(8,128)(2,1)} %get-tuple-element.56.refs_1_), channel_id=1, source_target_pairs={{0,12},{1,13},{2,14},{3,15},{4,0},{5,1},{6,2},{7,3},{8,4},{9,5},{1... | collective-permute-start | bytes 1105928 | tf_op jit(solution)/shard_map/ppermute | solution.py:34
  52.2 24.9 %collective-permute-start.14 = (bf16[160,1536]{1,0:T(8,128)(2,1)}, bf16[160,1536]{1,0:T(8,128)(2,1)S(1)}, u32[]{:S(2)}, u32[]{:S(2)}) collective-permute-start(bf16[160,1536]{1,0:T(8,128)(2,1)} %get-tuple-element.55.refs_1_), channel_id=1, source_target_pairs={{0,3},{1,0},{2,1},{3,2},{4,7},{5,4},{6,5},{7,6},{8,11},{9,8},{10,9... | collective-permute-start | bytes 1474568 | tf_op jit(solution)/shard_map/ppermute | solution.py:29
  53.5 23.6 %collective-permute-start.13 = (bf16[160,1152]{1,0:T(8,128)(2,1)}, bf16[160,1152]{1,0:T(8,128)(2,1)}, u32[]{:S(2)}, u32[]{:S(2)}) collective-permute-start(bf16[160,1152]{1,0:T(8,128)(2,1)} %get-tuple-element.56.refs_1_), channel_id=1, source_target_pairs={{0,4},{1,5},{2,6},{3,7},{4,8},{5,9},{6,10},{7,11},{8,12},{9,13},{1... | collective-permute-start | bytes 1105928 | tf_op jit(solution)/shard_map/ppermute | solution.py:34
  60.0 13.3 %copy-start.4 = (bf16[160,1152]{1,0:T(8,128)(2,1)}, bf16[160,1152]{1,0:T(8,128)(2,1)S(1)}, u32[]{:S(2)}) copy-start(bf16[160,1152]{1,0:T(8,128)(2,1)S(1)} %collective-permute-done.10.refs_3_) | copy-start | bytes 1105924
  69.2 17.5 %copy-start.2 = (bf16[160,1536]{1,0:T(8,128)(2,1)}, bf16[160,1536]{1,0:T(8,128)(2,1)S(1)}, u32[]{:S(2)}) copy-start(bf16[160,1536]{1,0:T(8,128)(2,1)S(1)} %collective-permute-done.9.refs_2_) | copy-start | bytes 1474564
  69.2 20.7 %collective-permute-start.12 = (bf16[160,1536]{1,0:T(8,128)(2,1)S(1)}, bf16[160,1536]{1,0:T(8,128)(2,1)}, u32[]{:S(2)}, u32[]{:S(2)}) collective-permute-start(bf16[160,1536]{1,0:T(8,128)(2,1)S(1)} %collective-permute-done.9.refs_2_), channel_id=1, source_target_pairs={{0,1},{1,2},{2,3},{3,0},{4,5},{5,6},{6,7},{7,4},{8,9},{9,10},{10,1... | collective-permute-start | bytes 1474568 | tf_op jit(solution)/shard_map/ppermute | solution.py:29
  69.2 20.7 %all-to-all-start.2 = ((bf16[4,160,512]{2,1,0:T(8,128)(2,1)}), bf16[4,160,512]{2,1,0:T(8,128)(2,1)}, u32[]{:S(2)}, u32[]{:S(2)}) async-start(bf16[4,160,512]{2,1,0:T(8,128)(2,1)} %get-tuple-element.86), calls=%async_computation.2 | async-start | bytes 1310720 | tf_op jit(solution)/shard_map/all_to_all | solution.py:42
  73.4 23.6 %collective-permute-start.15 = (bf16[4,160,1024]{2,1,0:T(8,128)(2,1)}, bf16[4,160,1024]{2,1,0:T(8,128)(2,1)}, u32[]{:S(2)}, u32[]{:S(2)}) collective-permute-start(bf16[4,160,1024]{2,1,0:T(8,128)(2,1)} %all-to-all-done.refs_4_), channel_id=1, source_target_pairs={{0,128},{128,0},{1,129},{129,1},{2,130},{130,2},{3,131},{131,3},{4... | collective-permute-start | bytes 3932168 | tf_op jit(solution)/shard_map/ppermute | solution.py:38
  74.2 15.7 %collective-permute-start.20 = (bf16[160,1152]{1,0:T(8,128)(2,1)}, bf16[160,1152]{1,0:T(8,128)(2,1)S(1)}, u32[]{:S(2)}, u32[]{:S(2)}) collective-permute-start(bf16[160,1152]{1,0:T(8,128)(2,1)} %copy-done.4), channel_id=1, source_target_pairs={{0,12},{1,13},{2,14},{3,15},{4,0},{5,1},{6,2},{7,3},{8,4},{9,5},{1... | collective-permute-start | bytes 1105928 | tf_op jit(solution)/shard_map/ppermute | solution.py:34
  77.2 9.6 %copy-start.3 = (bf16[160,1536]{1,0:T(8,128)(2,1)}, bf16[160,1536]{1,0:T(8,128)(2,1)S(1)}, u32[]{:S(2)}) copy-start(bf16[160,1536]{1,0:T(8,128)(2,1)S(1)} %collective-permute-done.14.refs_3_) | copy-start | bytes 1474564
  89.9 45.4 %all-to-all-start.1 = ((bf16[8,20,4096]{2,1,0:T(8,128)(2,1)}), bf16[8,20,4096]{2,1,0:T(8,128)(2,1)S(1)}, u32[]{:S(2)}, u32[]{:S(2)}) async-start(bf16[8,20,4096]{2,1,0:T(8,128)(2,1)} %shard_map.96), calls=%async_computation.1 | async-start | bytes 3145728 | tf_op jit(solution)/shard_map/all_to_all | solution.py:491
  94.9 10.8 %collective-permute-start.22 = (bf16[4,160,512]{2,1,0:T(8,128)(2,1)}, bf16[4,160,512]{2,1,0:T(8,128)(2,1)}, u32[]{:S(2)}, u32[]{:S(2)}) collective-permute-start(bf16[4,160,512]{2,1,0:T(8,128)(2,1)} %all-to-all-done.2.refs_4_), channel_id=1, source_target_pairs={{0,128},{128,0},{1,129},{129,1},{2,130},{130,2},{3,131},{131,3},{4... | collective-permute-start | bytes 1966088 | tf_op jit(solution)/shard_map/ppermute | solution.py:38
  102.8 12.0 %collective-permute-start.16 = (bf16[128,1536]{1,0:T(8,128)(2,1)S(1)}, bf16[128,1536]{1,0:T(8,128)(2,1)S(1)}, u32[]{:S(2)}, u32[]{:S(2)}) collective-permute-start(bf16[128,1536]{1,0:T(8,128)(2,1)S(1)} %get-tuple-element.71), channel_id=1, source_target_pairs={{0,4},{1,5},{2,6},{3,7},{4,8},{5,9},{6,10},{7,11},{8,12},{9,13},{1... | collective-permute-start | bytes 1179656 | tf_op jit(solution)/shard_map/ppermute | solution.py:34
  104.1 10.8 %collective-permute-start.17 = (bf16[128,1536]{1,0:T(8,128)(2,1)S(1)}, bf16[128,1536]{1,0:T(8,128)(2,1)S(1)}, u32[]{:S(2)}, u32[]{:S(2)}) collective-permute-start(bf16[128,1536]{1,0:T(8,128)(2,1)S(1)} %get-tuple-element.72), channel_id=1, source_target_pairs={{0,12},{1,13},{2,14},{3,15},{4,0},{5,1},{6,2},{7,3},{8,4},{9,5},{1... | collective-permute-start | bytes 1179656 | tf_op jit(solution)/shard_map/ppermute | solution.py:34
  110.1 10.5 %copy-start = (f32[256,1152]{1,0:T(8,128)}, f32[256,1152]{1,0:T(8,128)S(1)}, u32[]{:S(2)}) copy-start(f32[256,1152]{1,0:T(8,128)S(1)} %get-tuple-element.87.own) | copy-start | bytes 3538948
  110.1 9.3 %collective-permute-start.23 = (bf16[128,1152]{1,0:T(8,128)(2,1)S(1)}, bf16[128,1152]{1,0:T(8,128)(2,1)S(1)}, u32[]{:S(2)}, u32[]{:S(2)}) collective-permute-start(bf16[128,1152]{1,0:T(8,128)(2,1)S(1)} %get-tuple-element.90), channel_id=1, source_target_pairs={{0,1},{1,2},{2,3},{3,0},{4,5},{5,6},{6,7},{7,4},{8,9},{9,10},{10,1... | collective-permute-start | bytes 884744 | tf_op jit(solution)/shard_map/ppermute | solution.py:29
  110.3 9.1 %collective-permute-start.24 = (bf16[128,1152]{1,0:T(8,128)(2,1)S(1)}, bf16[128,1152]{1,0:T(8,128)(2,1)S(1)}, u32[]{:S(2)}, u32[]{:S(2)}) collective-permute-start(bf16[128,1152]{1,0:T(8,128)(2,1)S(1)} %get-tuple-element.91), channel_id=1, source_target_pairs={{0,3},{1,0},{2,1},{3,2},{4,7},{5,4},{6,5},{7,6},{8,11},{9,8},{10,9... | collective-permute-start | bytes 884744 | tf_op jit(solution)/shard_map/ppermute | solution.py:29
  116.1 20.0 %collective-permute-start.18 = (bf16[256,1536]{1,0:T(8,128)(2,1)}, bf16[256,1536]{1,0:T(8,128)(2,1)}, u32[]{:S(2)}, u32[]{:S(2)}) collective-permute-start(bf16[256,1536]{1,0:T(8,128)(2,1)} %get-tuple-element.73), channel_id=1, source_target_pairs={{0,4},{1,5},{2,6},{3,7},{4,8},{5,9},{6,10},{7,11},{8,12},{9,13},{1... | collective-permute-start | bytes 2359304 | tf_op jit(solution)/shard_map/ppermute | solution.py:34
  116.7 19.5 %collective-permute-start.19 = (bf16[256,1536]{1,0:T(8,128)(2,1)}, bf16[256,1536]{1,0:T(8,128)(2,1)}, u32[]{:S(2)}, u32[]{:S(2)}) collective-permute-start(bf16[256,1536]{1,0:T(8,128)(2,1)} %get-tuple-element.74), channel_id=1, source_target_pairs={{0,12},{1,13},{2,14},{3,15},{4,0},{5,1},{6,2},{7,3},{8,4},{9,5},{1... | collective-permute-start | bytes 2359304 | tf_op jit(solution)/shard_map/ppermute | solution.py:34
  120.6 18.8 %collective-permute-start.25 = (bf16[256,1152]{1,0:T(8,128)(2,1)}, bf16[256,1152]{1,0:T(8,128)(2,1)}, u32[]{:S(2)}, u32[]{:S(2)}) collective-permute-start(bf16[256,1152]{1,0:T(8,128)(2,1)} %get-tuple-element.92), channel_id=1, source_target_pairs={{0,1},{1,2},{2,3},{3,0},{4,5},{5,6},{6,7},{7,4},{8,9},{9,10},{10,1... | collective-permute-start | bytes 1769480 | tf_op jit(solution)/shard_map/ppermute | solution.py:29
  121.5 18.0 %collective-permute-start.26 = (bf16[256,1152]{1,0:T(8,128)(2,1)}, bf16[256,1152]{1,0:T(8,128)(2,1)}, u32[]{:S(2)}, u32[]{:S(2)}) collective-permute-start(bf16[256,1152]{1,0:T(8,128)(2,1)} %get-tuple-element.93), channel_id=1, source_target_pairs={{0,3},{1,0},{2,1},{3,2},{4,7},{5,4},{6,5},{7,6},{8,11},{9,8},{10,9... | collective-permute-start | bytes 1769480 | tf_op jit(solution)/shard_map/ppermute | solution.py:29
  136.2 3.3 %copy-start.1 = (f32[256,1152]{1,0:T(8,128)S(1)}, f32[256,1152]{1,0:T(8,128)}, u32[]{:S(2)}) copy-start(f32[256,1152]{1,0:T(8,128)} %copy-done) | copy-start | bytes 3538948
  137.9 4.7 %collective-permute-start.21 = (bf16[128,1536]{1,0:T(8,128)(2,1)S(1)}, bf16[128,1536]{1,0:T(8,128)(2,1)S(1)}, u32[]{:S(2)}, u32[]{:S(2)}) collective-permute-start(bf16[128,1536]{1,0:T(8,128)(2,1)S(1)} %get-tuple-element.84), channel_id=1, source_target_pairs={{0,128},{128,0},{1,129},{129,1},{2,130},{130,2},{3,131},{131,3},{4... | collective-permute-start | bytes 1179656 | tf_op jit(solution)/shard_map/ppermute | solution.py:38
  140.9 1.7 %collective-permute-start.27 = (bf16[128,1152]{1,0:T(8,128)(2,1)S(1)}, bf16[128,1152]{1,0:T(8,128)(2,1)S(1)}, u32[]{:S(2)}, u32[]{:S(2)}) collective-permute-start(bf16[128,1152]{1,0:T(8,128)(2,1)S(1)} %get-tuple-element.95), channel_id=1, source_target_pairs={{0,128},{128,0},{1,129},{129,1},{2,130},{130,2},{3,131},{131,3},{4... | collective-permute-start | bytes 884744 | tf_op jit(solution)/shard_map/ppermute | solution.py:38
